TPU v7x, 256 devices: a whole 4x4x8 slice. The times are simulated.
256 devices in a mesh: dp: 16 (over y, x), expert: 8 (over z), tensor: 2 (over core).
Axes of the slice: x: 4, y: 4, z: 8, core: 2. Of those that a mesh axis runs over, the one named last changes fastest.
Arguments:
- out_grad: bfloat16 [16384, 2048], P(('dp', 'expert'), 'tensor'), may hold values from -6 to 6
- seq_ids: int32 [128, 128], P(('dp', 'expert')), may hold values from 0 to 3, never falling along the last dimension, each value on 1 to 64 neighbouring positions
- seq_weights: float32 [128, 4], P(('dp', 'expert')), may hold values from -1.5 to 1.5
- expert_ids: int32 [16384, 2], P(('dp', 'expert')), may hold values from 0 to 7, all different within a row; in each aligned block of 128 rows (0 to 127, 128 to 255, ...) at most 48 rows name the same one
- route_probs: bfloat16 [16384, 2], P(('dp', 'expert')), may hold values from 0.19921875 to 1
- down_weight: bfloat16 [8, 7168, 2048], P('expert', ('dp', 'tensor')), may hold values from -0.0625 to 0.0625
- gate_pre: bfloat16 [8, 7168, 6144], P('expert', ('dp', 'tensor')), may hold values from -6 to 6
- up_pre: bfloat16 [8, 7168, 6144], P('expert', ('dp', 'tensor')), may hold values from -6 to 6
Outputs:
- grad_gate: bfloat16 [8, 7168, 6144], P('expert', ('dp', 'tensor'))
- grad_up: bfloat16 [8, 7168, 6144], P('expert', ('dp', 'tensor'))
- grad_down: bfloat16 [8, 7168, 2048], P('expert', ('dp', 'tensor'))
- grad_probs: float32 [16384, 2], P(('dp', 'expert'))
Inputs may be any that keep to these rules, and one draw needn't show every extreme that they name: `expert_ids`: the two experts of a token differ. Among the 128 tokens of one shard no expert is named more than 48 times, and in every draw some expert is named exactly 48 times by the tokens of some shard. `seq_ids`: along a shard's row the ids never fall; each of the 4 ids names 1 to 64 tokens of the row, and one names exactly 64.
All inputs are finite; a program needn't handle non-finite values.
Results may differ from a plain program's by a relative error of at most 0.0064.
Values may be sent and summed in bfloat16 or wider, within the bound.
No kernel may reach another device: no remote copies, remote signals or barrier semaphores. Data moves between devices by JAX's collectives and lax.ppermute only.
A program may use at most 128 MiB of HBM per device.

v0:
```python
import functools

import jax
import jax.numpy as jnp
import numpy as np
from jax import lax
from jax.experimental import pallas as pl
from jax.experimental.pallas import tpu as pltpu
from jax.sharding import PartitionSpec as P

SIDE = 4
NT = (((1,), (1,)), ((), ()))
VMEM = pl.BlockSpec(memory_space=pltpu.VMEM)
SMEM = pl.BlockSpec(memory_space=pltpu.SMEM)
ANY = pl.BlockSpec(memory_space=pl.ANY)


def params(mib=8):
    return pltpu.CompilerParams(vmem_limit_bytes=mib * 1024 * 1024)


def cost(flops=1000, bytes_accessed=1000):
    return pl.CostEstimate(flops=int(flops), bytes_accessed=int(bytes_accessed), transcendentals=0)


def pack_kernel(z_ref, grad_ref, seq_ref, sw_ref, ids_ref, probs_ref, *outs):
    *outs, slot_ref = outs
    experts, cap = len(outs), outs[0].shape[0]
    tokens = grad_ref.shape[0]
    seq = seq_ref[...]
    weight = jnp.zeros((1, tokens), jnp.float32)
    for j in range(sw_ref.shape[1]):
        weight = weight + jnp.where(seq == j, sw_ref[0, j], 0.0)
    z = z_ref[0]
    chosen = [ids_ref[k : k + 1, :] for k in range(2)]
    probs = [probs_ref[k : k + 1, :].astype(jnp.float32) for k in range(2)]
    expert_row = lax.broadcasted_iota(jnp.int32, (experts, tokens), 0)
    hits = [(c == expert_row).astype(jnp.float32) for c in chosen]
    before = lax.broadcasted_iota(jnp.int32, (tokens, tokens), 0) < lax.broadcasted_iota(
        jnp.int32, (tokens, tokens), 1
    )
    earlier = jnp.dot(
        (hits[0] + hits[1]).astype(jnp.bfloat16),
        before.astype(jnp.float32).astype(jnp.bfloat16),
        preferred_element_type=jnp.float32,
    )
    row = lax.broadcasted_iota(jnp.int32, (experts * cap, tokens), 0)
    pick = jnp.zeros((experts * cap, tokens), jnp.float32)
    prob = jnp.zeros((experts * cap, tokens), jnp.float32)
    for k in range(2):
        pos = jnp.sum(hits[k] * earlier, axis=0, keepdims=True).astype(jnp.int32)
        slot_ref[k : k + 1, :] = pos
        relative = lax.rem(chosen[k] - z + experts, experts) * cap + pos
        mine = row == relative
        pick = jnp.where(mine, 1.0, pick)
        prob = jnp.where(mine, probs[k], prob)
    slot_weight = jnp.sum(pick * weight, axis=1, keepdims=True)
    slot_prob = jnp.sum(prob, axis=1, keepdims=True)
    rows = jnp.dot(pick.astype(jnp.bfloat16), grad_ref[...], preferred_element_type=jnp.float32)
    rows = (slot_weight * rows).astype(jnp.bfloat16).astype(jnp.float32)
    rows = (slot_prob * rows).astype(jnp.bfloat16)
    for k in range(experts):
        outs[k][...] = rows[k * cap : (k + 1) * cap]


def pack(z, grad, seq, sw, ids, probs, experts, cap):
    tokens, width = grad.shape
    return pl.pallas_call(
        pack_kernel,
        in_specs=[SMEM, VMEM, VMEM, SMEM, VMEM, VMEM],
        out_specs=[VMEM] * (experts + 1),
        out_shape=[jax.ShapeDtypeStruct((cap, width), jnp.bfloat16)] * experts
        + [jax.ShapeDtypeStruct((2, tokens), jnp.int32)],
        compiler_params=params(),
        cost_estimate=cost(),
        name="pack",
    )(z, grad, seq, sw, ids, probs)


def unpack_kernel(table_ref, ids_ref, pos_ref, probs_ref, out_ref):
    experts, cap = table_ref.shape
    tokens = ids_ref.shape[1]
    expert_row = lax.broadcasted_iota(jnp.int32, (experts, tokens), 0)
    cap_row = lax.broadcasted_iota(jnp.int32, (cap, tokens), 0)
    for k in range(2):
        at = (pos_ref[k : k + 1, :] == cap_row).astype(jnp.float32)
        values = jnp.dot(
            table_ref[...], at, preferred_element_type=jnp.float32,
            precision=lax.Precision.HIGHEST,
        )
        value = jnp.sum(
            jnp.where(ids_ref[k : k + 1, :] == expert_row, values, 0.0), axis=0, keepdims=True
        )
        out_ref[k : k + 1, :] = value / probs_ref[k : k + 1, :].astype(jnp.float32)


def unpack(table, ids, pos, probs):
    return pl.pallas_call(
        unpack_kernel,
        in_specs=[VMEM] * 4,
        out_specs=VMEM,
        out_shape=jax.ShapeDtypeStruct(ids.shape, jnp.float32),
        compiler_params=params(),
        name="unpack",
    )(table, ids, pos, probs)


def prepare_kernel(ids_ref, gate_ref, up_ref, w_ref, slope_ref, act_ref, hidden_ref, half_ref):
    gate = gate_ref[...].astype(jnp.float32)
    up = up_ref[...].astype(jnp.float32)
    logistic = 1.0 / (1.0 + jnp.exp(-gate))
    activated = gate * logistic
    slope_ref[...] = (up * logistic * (1.0 + gate * (1.0 - logistic))).astype(jnp.bfloat16)
    act_ref[...] = activated.astype(jnp.bfloat16)
    hidden_ref[...] = (activated * up).astype(jnp.bfloat16)
    half_ref[...] = w_ref[...]


def prepare(ids, gate, up, weight):
    f, slots = gate.shape
    width = weight.shape[1] // 2
    step = 32
    columns = ids.shape[0] - 1
    spec = pl.BlockSpec((step, slots), lambda i, ids: (i, 0))
    return pl.pallas_call(
        prepare_kernel,
        grid_spec=pltpu.PrefetchScalarGridSpec(
            num_scalar_prefetch=1,
            grid=(f // step,),
            in_specs=[
                spec, spec, pl.BlockSpec((step, width), lambda i, ids: (i, 1 - ids[columns]))
            ],
            out_specs=[spec] * 3 + [pl.BlockSpec((step, width), lambda i, ids: (i, 0))],
        ),
        out_shape=[jax.ShapeDtypeStruct(gate.shape, jnp.bfloat16)] * 3
        + [jax.ShapeDtypeStruct((f, width), jnp.bfloat16)],
        compiler_params=params(10),
        cost_estimate=cost(4000 * 1000 * 1000, 10 * f * slots),
        name="prepare",
    )(ids, gate, up, weight)


def order_kernel(e_ref, *refs):
    *chunks, out = refs
    experts, cap = len(chunks), chunks[0].shape[0]
    for k in range(experts):
        source = lax.rem(e_ref[0] - k + experts, experts)
        out[pl.ds(pl.multiple_of(source * cap, 16), cap), :] = chunks[k][...]


def in_order(e, chunks):
    cap, width = chunks[0].shape
    rows = cap * len(chunks)
    return pl.pallas_call(
        order_kernel,
        in_specs=[SMEM] + [VMEM] * len(chunks),
        out_specs=VMEM,
        out_shape=jax.ShapeDtypeStruct((rows, width), jnp.bfloat16),
        compiler_params=params(),
        cost_estimate=cost(),
        name="in_order",
    )(e, *chunks)


def shifts(first, second):
    pairs = []
    for y in range(SIDE):
        for x in range(SIDE):
            me = y * SIDE + x
            a = ((y + second) % SIDE) * SIDE + (x + first) % SIDE
            b = ((y + first) % SIDE) * SIDE + (x + second) % SIDE
            pairs += [(2 * me, 2 * a), (2 * me + 1, 2 * b + 1)]
    return pairs


def hop(array, first, second):
    return lax.ppermute(array, ("dp", "tensor"), shifts(first, second))


def swap(array):
    return lax.ppermute(array, "tensor", [(0, 1), (1, 0)])


def other_kernel(w_ref, *refs):
    *blocks, out = refs
    for i, block in enumerate(blocks):
        out[i] = lax.dot_general(
            w_ref[...], block[...], NT, preferred_element_type=jnp.float32
        ).astype(jnp.bfloat16)


def for_other(weight, blocks):
    f, width = weight.shape
    rows = blocks[0].shape[0]
    n = len(blocks)
    return pl.pallas_call(
        other_kernel,
        in_specs=[VMEM] * (n + 1),
        out_specs=VMEM,
        out_shape=jax.ShapeDtypeStruct((n, f, rows), jnp.bfloat16),
        compiler_params=params(10),
        cost_estimate=cost(),
        name="for_other",
    )(weight, *blocks)


def down_kernel(n, start, first, last, ids_ref, own_ref, other_ref, *refs):
    blocks, refs = refs[:n], refs[n:]
    both = refs[-1]
    f = own_ref.shape[0]
    rows, width = blocks[0].shape
    for j in range(n):
        column = pl.ds(pl.multiple_of(ids_ref[start + j] * rows, 128), rows)
        both[:f, j * rows : (j + 1) * rows] = own_ref[:, column]
        both[f:, j * rows : (j + 1) * rows] = other_ref[:, column]
    tile = 512

    @pl.loop(0, width // tile)
    def _(t):
        part = pl.ds(pl.multiple_of(t * tile, tile), tile)
        total = jnp.dot(
            both[...],
            jnp.concatenate([block[:, part] for block in blocks], axis=0),
            preferred_element_type=jnp.float32,
        )
        if not first:
            total = total + refs[0][:, part]
        if last:
            mine_ref, theirs_ref = refs[1 - first : 3 - first]
            mine_ref[:, part] = total[:f].astype(jnp.bfloat16)
            theirs_ref[:, part] = total[f:].astype(jnp.bfloat16)
        else:
            refs[1 - first][:, part] = total


def down(ids, start, own, other, blocks, acc, last):
    f = own.shape[0]
    rows, width = blocks[0].shape
    n = len(blocks)
    first = acc is None
    half = jax.ShapeDtypeStruct((f, width), jnp.bfloat16)
    return pl.pallas_call(
        functools.partial(down_kernel, n, start, first, last),
        in_specs=[SMEM] + [VMEM] * (2 + n + (not first)),
        out_specs=[VMEM, VMEM] if last else VMEM,
        out_shape=[half, half] if last else jax.ShapeDtypeStruct((2 * f, width), jnp.float32),
        scratch_shapes=[pltpu.VMEM((2 * f, n * rows), jnp.bfloat16)],
        compiler_params=params(16),
        cost_estimate=cost(2000 * 1000 * 1000, 1000) if last else cost(),
        name="down",
    )(ids, in_vmem(own), in_vmem(other), *blocks, *([] if first else [acc]))


def finish_kernel(ids_ref, mine_ref, theirs_ref, out_ref):
    core = ids_ref[ids_ref.shape[0] - 1]
    width = mine_ref.shape[1]
    out_ref[:, pl.ds(pl.multiple_of(core * width, 128), width)] = mine_ref[...]
    out_ref[:, pl.ds(pl.multiple_of((1 - core) * width, 128), width)] = theirs_ref[...]


def finish(ids, mine, theirs):
    f, width = mine.shape
    return pl.pallas_call(
        finish_kernel,
        in_specs=[SMEM, VMEM, VMEM],
        out_specs=VMEM,
        out_shape=jax.ShapeDtypeStruct((f, 2 * width), mine.dtype),
        compiler_params=params(),
        cost_estimate=cost(),
        name="finish",
    )(ids, mine, theirs)


def act_kernel(n, start, where, groups, ids_ref, w_ref, slope_ref, act_ref, hidden_ref, *refs):
    blocks, parts = refs[:n], refs[n : n + groups]
    gate_out, up_out, probe_out, gate_buf, up_buf, weight, sems = refs[-7:]
    rows, width = blocks[0].shape
    core = ids_ref[ids_ref.shape[0] - 1]
    load = pltpu.make_async_copy(
        w_ref.at[:, pl.ds(pl.multiple_of(core * width, 128), width)], weight, sems.at[2, 0]
    )
    load.start()
    load.wait()

    def copies(j):
        column = pl.ds(pl.multiple_of(ids_ref[start + j] * rows, 128), rows)
        return (
            pltpu.make_async_copy(gate_buf.at[j], gate_out.at[:, column], sems.at[0, j]),
            pltpu.make_async_copy(up_buf.at[j], up_out.at[:, column], sems.at[1, j]),
        )

    for j in range(n):
        upstream = lax.dot_general(
            weight[...], blocks[j][...], NT, preferred_element_type=jnp.float32
        )
        group, at = where[j]
        upstream = upstream + parts[group][at].astype(jnp.float32)
        column = pl.ds(pl.multiple_of(ids_ref[start + j] * rows, 128), rows)
        gate_buf[j] = (upstream * slope_ref[:, column].astype(jnp.float32)).astype(jnp.bfloat16)
        up_buf[j] = (upstream * act_ref[:, column].astype(jnp.float32)).astype(jnp.bfloat16)
        for copy in copies(j):
            copy.start()
        probe_out[ids_ref[start + j]] = jnp.sum(
            upstream * hidden_ref[:, column].astype(jnp.float32), axis=0, keepdims=True
        )
    for j in range(n):
        for copy in copies(j):
            copy.wait()


def act(ids, start, weight, slope, activated, hidden, blocks, parts, where, held):
    f, slots = slope.shape
    rows = blocks[0].shape[0]
    n, groups = len(blocks), len(parts)
    first = held is None
    base = 5 + n + groups
    return pl.pallas_call(
        functools.partial(act_kernel_first if first else act_kernel_next, n, start, where, groups),
        in_specs=[SMEM, ANY] + [VMEM] * (3 + n + groups) + ([] if first else [ANY, ANY, VMEM]),
        out_specs=[ANY, ANY, VMEM],
        out_shape=[
            jax.ShapeDtypeStruct((f, slots), jnp.bfloat16),
            jax.ShapeDtypeStruct((f, slots), jnp.bfloat16),
            jax.ShapeDtypeStruct((slots // rows, 1, rows), jnp.float32),
        ],
        scratch_shapes=[
            pltpu.VMEM((n, f, rows), jnp.bfloat16),
            pltpu.VMEM((n, f, rows), jnp.bfloat16),
            pltpu.VMEM((f, blocks[0].shape[1]), jnp.bfloat16),
            pltpu.SemaphoreType.DMA((3, n)),
        ],
        input_output_aliases={} if first else {base: 0, base + 1: 1},
        compiler_params=params(16),
        cost_estimate=cost(),
        name="act",
    )(ids, in_hbm(weight), in_vmem(slope), in_vmem(activated), in_vmem(hidden), *blocks, *parts, *([] if first else held))


def act_kernel_first(*args):
    act_kernel(*args)


def act_kernel_next(n, start, where, groups, *refs):
    inputs = refs[: 5 + n + groups]
    held_probe, probe_out = refs[5 + n + groups + 2], refs[-5]
    probe_out[...] = held_probe[...]
    act_kernel(n, start, where, groups, *inputs, *refs[-7:])


def in_hbm(array):
    return pltpu.with_memory_space_constraint(array, pltpu.HBM)


def in_vmem(array):
    return pltpu.with_memory_space_constraint(array, pltpu.VMEM)


def after(array, *others):
    return lax.optimization_barrier((array, *others))[0]


ACT = (
    ((0, 0), (1, 0), (-1, 0), (0, 1), (0, -1)),
    ((1, 1), (1, -1), (-1, 1), (-1, -1)),
    ((2, 0), (0, 2), (2, 1), (1, 2)),
    ((-1, 2), (2, -1), (2, 2)),
)
OTHER = (
    ((0, 0), (1, 0), (-1, 0), (0, 1), (0, -1)),
    ((2, 0), (1, 1), (1, -1)),
    ((-1, 1), (-1, -1), (2, 1), (2, -1)),
    ((0, 2), (1, 2)),
    ((-1, 2), (2, 2)),
)
LABELS = sum(ACT, ())
PLACE = {label: (g, i) for g, labels in enumerate(OTHER) for i, label in enumerate(labels)}


def index_table():
    table = np.zeros((2 * SIDE * SIDE, len(LABELS) + 1), np.int32)
    for device in range(2 * SIDE * SIDE):
        core, x, y = device % 2, device // 2 % SIDE, device // 2 // SIDE
        for i, (first, second) in enumerate(LABELS):
            dx, dy = (second, first) if core else (first, second)
            table[device, i] = (y - dy) % SIDE * SIDE + (x - dx) % SIDE
        table[device, -1] = core
    return table


def local(out_grad, seq_ids, seq_weights, expert_ids, route_probs, down_weight, gate_pre, up_pre):
    experts = lax.axis_size("expert")
    columns = lax.axis_size("dp")
    width = out_grad.shape[1]
    cap = gate_pre.shape[2] // (columns * experts)
    rows = experts * cap
    weight = down_weight[0]
    core = lax.axis_index("tensor")
    e_arr = lax.axis_index("expert").reshape(1).astype(jnp.int32)
    ids = lax.dynamic_index_in_dim(
        jnp.asarray(index_table()), lax.axis_index("dp") * 2 + core, 0, keepdims=False
    )

    *sent, pos = pack(
        after(e_arr, ids), in_hbm(out_grad), in_hbm(seq_ids), seq_weights, in_hbm(expert_ids.T),
        in_hbm(route_probs.T), experts, cap
    )
    chunks = [sent[0]] + [
        lax.ppermute(sent[k], "expert", [(i, (i + k) % experts) for i in range(experts)])
        for k in range(1, experts)
    ]
    slope, activated, hidden, w_send = prepare(
        ids, in_hbm(gate_pre[0]), in_hbm(after(up_pre[0], pos)), in_hbm(weight)
    )
    block = in_order(after(e_arr, hidden), [in_hbm(c) for c in chunks])
    w_other = swap(after(w_send, block))
    hidden_other = swap(after(hidden, block))

    b = {(0, 0): block}
    parts, held = [], None

    def other():
        parts.append(swap(for_other(w_other, [b[l] for l in OTHER[len(parts)]])))

    def activate(step, held):
        labels = ACT[step]
        need = sorted({PLACE[s, f][0] for f, s in labels})
        where = [(need.index(PLACE[s, f][0]), PLACE[s, f][1]) for f, s in labels]
        start = sum(len(a) for a in ACT[:step])
        return act(
            ids, start, weight, slope, activated, hidden, [b[l] for l in labels],
            [parts[g] for g in need], where, held,
        )

    def send_both(first, source):
        b[first, 1] = hop(source, 0, 1)
        b[first, -1] = hop(source, 0, -1)

    b[1, 0] = hop(block, 1, 0)
    b[-1, 0] = hop(block, -1, 0)
    send_both(0, block)
    b[2, 0] = hop(b[1, 0], 1, 0)
    send_both(1, b[1, 0])
    send_both(-1, after(b[-1, 0], b[0, 1], b[0, -1]))
    raw = for_other(w_other, [b[l] for l in OTHER[0]])
    parts.append(swap(raw))
    send_both(2, after(b[2, 0], raw, b[1, 1], b[1, -1]))
    held = activate(0, held)
    b[0, 2] = hop(after(b[0, 1], b[-1, 1], held[2]), 0, 1)
    b[1, 2] = hop(after(b[1, -1], b[-1, 1], held[2]), 0, -1)
    raw = for_other(w_other, [b[l] for l in OTHER[1]])
    parts.append(swap(raw))
    acc = down(ids, 0, hidden, hidden_other, [b[l] for l in ACT[0]], None, False)
    b[-1, 2] = hop(after(b[-1, 1], raw, acc, b[2, 1]), 0, 1)
    b[2, 2] = hop(after(b[2, -1], raw, acc, b[2, 1]), 0, -1)
    raw = for_other(w_other, [b[l] for l in OTHER[2]])
    parts.append(swap(raw))
    held = activate(1, held)
    raw = for_other(w_other, [b[l] for l in OTHER[3]])
    parts.append(swap(raw))
    held = activate(2, held)
    middle = ACT[1] + ACT[2]
    acc = down(ids, len(ACT[0]), hidden, hidden_other, [b[l] for l in middle], acc, False)
    last = after(b[-1, 2], held[2], acc)
    raw = for_other(w_other, [last, b[2, 2]])
    parts.append(swap(raw))
    blocks = [after(b[ACT[3][0]], raw)] + [b[l] for l in ACT[3][1:]]
    mine, theirs = down(
        ids, len(ACT[0] + middle), hidden, hidden_other, blocks, acc, True
    )
    gate_out, up_out, probe = activate(3, held)
    grad_down = finish(ids, mine, swap(after(theirs, probe)))

    shared = jnp.sum(lax.all_to_all(probe.reshape(columns, rows), "dp", 0, 0, tiled=True), axis=0)
    totals = lax.all_gather(shared, "tensor").sum(0)
    returned = lax.all_to_all(totals.reshape(experts, cap), "expert", 0, 0, tiled=True)
    grad_probs = unpack(returned, expert_ids.T, pos, route_probs.T).T
    return gate_out[None], up_out[None], grad_down[None], grad_probs


def solution(mesh):
    return jax.shard_map(
        local,
        mesh=mesh,
        in_specs=(
            P(("dp", "expert"), "tensor"),
            P(("dp", "expert"), None),
            P(("dp", "expert"), None),
            P(("dp", "expert"), None),
            P(("dp", "expert"), None),
            P("expert", ("dp", "tensor"), None),
            P("expert", ("dp", "tensor"), None),
            P("expert", ("dp", "tensor"), None),
        ),
        out_specs=(
            P("expert", ("dp", "tensor"), None),
            P("expert", ("dp", "tensor"), None),
            P("expert", ("dp", "tensor"), None),
            P(("dp", "expert"), None),
        ),
        check_vma=False,
    )
```

profile of v0, /device:TPU:1, one launch (start us, length us, event | category | flops | bytes accessed | tf_op | source)
XLA Modules:
  0.0 158.2 jit_solution(2388014389863712172)
XLA Ops:
  0.6 0.7 dynamic-slice_bitcast_fusion.ids_ref.args_0_.refs_0_
  1.3 0.7 copy-done.3
  2.0 1.5 pack.1
  3.5 0.6 copy-done
  4.2 2.5 %collective-permute-start = (bf16[48,1024]{1,0:T(8,128)(2,1)S(1)}, bf16[48,1024]{1,0:T(8,128)(2,1)S(1)}, u32[]{:S(2)}, u32[]{:S(2)}) collective-permute-start(bf16[48,1024]{1,0:T(8,128)(2,1)S(1)} %get-tuple-element.53), channel_id=1, source_target_pairs={{0,2},{2,4},{4,6},{6,8},{8,10},{10,12},{12,14},{14,0},{1,3},{3,5},... | collective-permute-start | bytes 294920 | tf_op jit(solution)/shard_map/ppermute | solution.py:408
  6.6 3.0 %collective-permute-start.1 = (bf16[48,1024]{1,0:T(8,128)(2,1)S(1)}, bf16[48,1024]{1,0:T(8,128)(2,1)S(1)}, u32[]{:S(2)}, u32[]{:S(2)}) collective-permute-start(bf16[48,1024]{1,0:T(8,128)(2,1)S(1)} %get-tuple-element.54), channel_id=1, source_target_pairs={{0,4},{2,6},{4,8},{6,10},{8,12},{10,14},{12,0},{14,2},{1,5},{3,7},... | collective-permute-start | bytes 294920 | tf_op jit(solution)/shard_map/ppermute | solution.py:408
  9.6 3.8 %collective-permute-start.2 = (bf16[48,1024]{1,0:T(8,128)(2,1)S(1)}, bf16[48,1024]{1,0:T(8,128)(2,1)S(1)}, u32[]{:S(2)}, u32[]{:S(2)}) collective-permute-start(bf16[48,1024]{1,0:T(8,128)(2,1)S(1)} %get-tuple-element.55), channel_id=1, source_target_pairs={{0,6},{2,8},{4,10},{6,12},{8,14},{10,0},{12,2},{14,4},{1,7},{3,9},... | collective-permute-start | bytes 294920 | tf_op jit(solution)/shard_map/ppermute | solution.py:408
  13.4 0.5 collective-permute-start.3
  13.8 4.5 %collective-permute-start.4 = (bf16[48,1024]{1,0:T(8,128)(2,1)S(1)}, bf16[48,1024]{1,0:T(8,128)(2,1)S(1)}, u32[]{:S(2)}, u32[]{:S(2)}) collective-permute-start(bf16[48,1024]{1,0:T(8,128)(2,1)S(1)} %get-tuple-element.57), channel_id=1, source_target_pairs={{0,10},{2,12},{4,14},{6,0},{8,2},{10,4},{12,6},{14,8},{1,11},{3,13... | collective-permute-start | bytes 294920 | tf_op jit(solution)/shard_map/ppermute | solution.py:408
  18.3 2.4 %collective-permute-start.5 = (bf16[48,1024]{1,0:T(8,128)(2,1)S(1)}, bf16[48,1024]{1,0:T(8,128)(2,1)S(1)}, u32[]{:S(2)}, u32[]{:S(2)}) collective-permute-start(bf16[48,1024]{1,0:T(8,128)(2,1)S(1)} %get-tuple-element.58), channel_id=1, source_target_pairs={{0,12},{2,14},{4,0},{6,2},{8,4},{10,6},{12,8},{14,10},{1,13},{3,15... | collective-permute-start | bytes 294920 | tf_op jit(solution)/shard_map/ppermute | solution.py:408
  20.7 0.7 collective-permute-start.6
  21.4 7.0 %prepare.1 = (bf16[224,6144]{1,0:T(8,128)(2,1)S(1)}, bf16[224,6144]{1,0:T(8,128)(2,1)S(1)}, bf16[224,6144]{1,0:T(8,128)(2,1)S(1)}, bf16[224,1024]{1,0:T(8,128)(2,1)S(1)}) custom-call(s32[17]{0:T(128)S(1)} %dynamic-slice_bitcast_fusion.ids_ref.args_0_.refs_0_, bf16[224,6144]{1,0:T(8,128)(2,1)} %bitcast.27, bf16[224,6144]{1,0:T(8,128)(2,1)} %bitcast.28, ...), custom_call_target="tpu_custom_call" | custom-call | flops 4000000000 | bytes 13762560 | tf_op jit(solution)/shard_map/prepare/pallas_call | solution.py:125
  28.5 4.7 %collective-permute-done.5.refs_6_ = bf16[48,1024]{1,0:T(8,128)(2,1)S(1)} collective-permute-done((bf16[48,1024]{1,0:T(8,128)(2,1)S(1)}, bf16[48,1024]{1,0:T(8,128)(2,1)S(1)}, u32[]{:S(2)}, u32[]{:S(2)}) %collective-permute-start.5) | collective-permute-done | bytes 98336 | tf_op jit(solution)/shard_map/ppermute | solution.py:408
  33.2 0.9 collective-permute-done.6.refs_7_
  34.1 0.6 copy-done.10
  34.7 1.3 in_order.1.refs_0_.args_5_
  36.0 0.7 collective-permute-start.16
  36.7 1.3 collective-permute-start.12
  38.0 0.3 collective-permute-start.11
  38.3 2.2 %collective-permute-start.9 = (bf16[384,1024]{1,0:T(8,128)(2,1)S(1)}, bf16[384,1024]{1,0:T(8,128)(2,1)S(1)}, u32[]{:S(2)}, u32[]{:S(2)}) collective-permute-start(bf16[384,1024]{1,0:T(8,128)(2,1)S(1)} %in_order.1.refs_0_.args_5_), channel_id=1, source_target_pairs={{0,192},{1,49},{16,208},{17,1},{32,224},{33,17},{48,240},{49,33},{... | collective-permute-start | bytes 2359304 | tf_op jit(solution)/shard_map/ppermute | solution.py:177
  40.5 1.6 %collective-permute-done.11.w_ref = bf16[224,1024]{1,0:T(8,128)(2,1)S(1)} collective-permute-done((bf16[224,1024]{1,0:T(8,128)(2,1)S(1)}, bf16[224,1024]{1,0:T(8,128)(2,1)S(1)}, u32[]{:S(2)}, u32[]{:S(2)}) %collective-permute-start.11) | collective-permute-done | bytes 458784 | tf_op jit(solution)/shard_map/ppermute | solution.py:181
  42.1 2.7 %collective-permute-start.7 = (bf16[384,1024]{1,0:T(8,128)(2,1)S(1)}, bf16[384,1024]{1,0:T(8,128)(2,1)S(1)}, u32[]{:S(2)}, u32[]{:S(2)}) collective-permute-start(bf16[384,1024]{1,0:T(8,128)(2,1)S(1)} %in_order.1.refs_0_.args_5_), channel_id=1, source_target_pairs={{0,48},{1,193},{16,0},{17,209},{32,16},{33,225},{48,32},{49,241},{... | collective-permute-start | bytes 2359304 | tf_op jit(solution)/shard_map/ppermute | solution.py:177
  44.8 7.6 %collective-permute-done.12.refs_1_.args_6_ = bf16[384,1024]{1,0:T(8,128)(2,1)S(1)} collective-permute-done((bf16[384,1024]{1,0:T(8,128)(2,1)S(1)}, bf16[384,1024]{1,0:T(8,128)(2,1)S(1)}, u32[]{:S(2)}, u32[]{:S(2)}) %collective-permute-start.12) | collective-permute-done | bytes 786464 | tf_op jit(solution)/shard_map/ppermute | solution.py:177
  52.5 3.5 %collective-permute-start.15 = (bf16[384,1024]{1,0:T(8,128)(2,1)S(1)}, bf16[384,1024]{1,0:T(8,128)(2,1)S(1)}, u32[]{:S(2)}, u32[]{:S(2)}) collective-permute-start(bf16[384,1024]{1,0:T(8,128)(2,1)S(1)} %collective-permute-done.12.refs_1_.args_6_), channel_id=1, source_target_pairs={{0,192},{1,49},{16,208},{17,1},{32,224},{33,17},{48,240},{49,33},{... | collective-permute-start | bytes 2359304 | tf_op jit(solution)/shard_map/ppermute | solution.py:177
  56.0 1.8 %collective-permute-done.8.refs_3_.args_8_ = bf16[384,1024]{1,0:T(8,128)(2,1)S(1)} collective-permute-done((bf16[384,1024]{1,0:T(8,128)(2,1)S(1)}, bf16[384,1024]{1,0:T(8,128)(2,1)S(1)}, u32[]{:S(2)}, u32[]{:S(2)}) %collective-permute-start.8) | collective-permute-done | bytes 786464 | tf_op jit(solution)/shard_map/ppermute | solution.py:177
  57.7 1.3 collective-permute-start.13
  59.0 1.4 for_other.6
  60.5 1.9 %collective-permute-start.23 = (bf16[5,224,384]{2,1,0:T(8,128)(2,1)S(1)}, bf16[5,224,384]{2,1,0:T(8,128)(2,1)S(1)}, u32[]{:S(2)}, u32[]{:S(2)}) collective-permute-start(bf16[5,224,384]{2,1,0:T(8,128)(2,1)S(1)} %for_other.6), channel_id=1, source_target_pairs={{0,1},{1,0},{2,3},{3,2},{4,5},{5,4},{6,7},{7,6},{8,9},{9,8},{10,11... | collective-permute-start | bytes 2580488 | tf_op jit(solution)/shard_map/ppermute | solution.py:181
  62.4 3.9 %collective-permute-done.15.refs_2_.refs_6_.refs_1_ = bf16[384,1024]{1,0:T(8,128)(2,1)S(1)} collective-permute-done((bf16[384,1024]{1,0:T(8,128)(2,1)S(1)}, bf16[384,1024]{1,0:T(8,128)(2,1)S(1)}, u32[]{:S(2)}, u32[]{:S(2)}) %collective-permute-start.15) | collective-permute-done | bytes 786464 | tf_op jit(solution)/shard_map/ppermute | solution.py:177
  66.3 1.2 collective-permute-start.10
  67.5 5.6 %collective-permute-done.14.refs_1_.refs_5_.refs_0_ = bf16[384,1024]{1,0:T(8,128)(2,1)S(1)} collective-permute-done((bf16[384,1024]{1,0:T(8,128)(2,1)S(1)}, bf16[384,1024]{1,0:T(8,128)(2,1)S(1)}, u32[]{:S(2)}, u32[]{:S(2)}) %collective-permute-start.14) | collective-permute-done | bytes 786464 | tf_op jit(solution)/shard_map/ppermute | solution.py:177
  73.0 3.9 %collective-permute-done.13.refs_0_.refs_5_.refs_4_ = bf16[384,1024]{1,0:T(8,128)(2,1)S(1)} collective-permute-done((bf16[384,1024]{1,0:T(8,128)(2,1)S(1)}, bf16[384,1024]{1,0:T(8,128)(2,1)S(1)}, u32[]{:S(2)}, u32[]{:S(2)}) %collective-permute-start.13) | collective-permute-done | bytes 786464 | tf_op jit(solution)/shard_map/ppermute | solution.py:177
  76.9 2.7 %collective-permute-start.19 = (bf16[384,1024]{1,0:T(8,128)(2,1)S(1)}, bf16[384,1024]{1,0:T(8,128)(2,1)S(1)}, u32[]{:S(2)}, u32[]{:S(2)}) collective-permute-start(bf16[384,1024]{1,0:T(8,128)(2,1)S(1)} %collective-permute-done.13.refs_0_.refs_5_.refs_4_), channel_id=1, source_target_pairs={{0,192},{1,49},{16,208},{17,1},{32,224},{33,17},{48,240},{49,33},{... | collective-permute-start | bytes 2359304 | tf_op jit(solution)/shard_map/ppermute | solution.py:177
  79.6 0.0 collective-permute-start.21
  79.7 4.4 %act.4 = (bf16[224,6144]{1,0:T(8,128)(2,1)}, bf16[224,6144]{1,0:T(8,128)(2,1)}, f32[16,1,384]{2,1,0:T(1,128)S(1)}) custom-call(s32[17]{0:T(128)S(1)} %dynamic-slice_bitcast_fusion.ids_ref.args_0_.refs_0_, bf16[224,2048]{1,0:T(8,128)(2,1)} %bitcast.21, bf16[224,6144]{1,0:T(8,128)(2,1)S(1)} %get-tuple-element.48.args_2_.refs_2_, ...), custom_call_target="tpu_custom_call" | custom-call | flops 1000 | bytes 1000 | tf_op jit(solution)/shard_map/act/pallas_call | solution.py:317
  84.0 1.1 collective-permute-done.10.refs_0_.refs_7_.refs_2_
  85.2 0.4 collective-permute-start.24
  85.5 2.3 %collective-permute-start.25 = (bf16[384,1024]{1,0:T(8,128)(2,1)S(1)}, bf16[384,1024]{1,0:T(8,128)(2,1)S(1)}, u32[]{:S(2)}, u32[]{:S(2)}) collective-permute-start(bf16[384,1024]{1,0:T(8,128)(2,1)S(1)} %collective-permute-done.15.refs_2_.refs_6_.refs_1_), channel_id=1, source_target_pairs={{0,192},{1,49},{16,208},{17,1},{32,224},{33,17},{48,240},{49,33},{... | collective-permute-start | bytes 2359304 | tf_op jit(solution)/shard_map/ppermute | solution.py:177
  87.8 0.9 for_other.5
  88.8 3.0 %down.3.refs_8_ = f32[448,1024]{1,0:T(8,128)S(1)} custom-call(s32[17]{0:T(128)S(1)} %dynamic-slice_bitcast_fusion.ids_ref.args_0_.refs_0_, bf16[224,6144]{1,0:T(8,128)(2,1)S(1)} %get-tuple-element.63.own_ref.args_4_.refs_4_, bf16[224,6144]{1,0:T(8,128)(2,1)S(1)} %collective-permute-done.16.other_ref, bf16[384,1024]{1,0:T(8,128)(2,1)S(1)} %in_order.1.refs_0_.args_5_, ...), custom_call_target="tpu_custom_call" | custom-call | flops 1000 | bytes 1000 | tf_op jit(solution)/shard_map/down/pallas_call | solution.py:242
  91.7 1.8 %collective-permute-done.17.refs_2_.refs_7_.refs_6_ = bf16[384,1024]{1,0:T(8,128)(2,1)S(1)} collective-permute-done((bf16[384,1024]{1,0:T(8,128)(2,1)S(1)}, bf16[384,1024]{1,0:T(8,128)(2,1)S(1)}, u32[]{:S(2)}, u32[]{:S(2)}) %collective-permute-start.17) | collective-permute-done | bytes 786464 | tf_op jit(solution)/shard_map/ppermute | solution.py:177
  93.6 2.7 %collective-permute-start.20 = (bf16[384,1024]{1,0:T(8,128)(2,1)S(1)}, bf16[384,1024]{1,0:T(8,128)(2,1)S(1)}, u32[]{:S(2)}, u32[]{:S(2)}) collective-permute-start(bf16[384,1024]{1,0:T(8,128)(2,1)S(1)} %collective-permute-done.19.refs_3_.refs_6_.refs_1_), channel_id=1, source_target_pairs={{0,192},{1,49},{16,208},{17,1},{32,224},{33,17},{48,240},{49,33},{... | collective-permute-start | bytes 2359304 | tf_op jit(solution)/shard_map/ppermute | solution.py:177
  96.3 0.7 collective-permute-done.21.refs_1_.refs_8_.refs_3_
  97.0 1.2 for_other.7
  98.2 5.3 %collective-permute-start.22 = (bf16[4,224,384]{2,1,0:T(8,128)(2,1)S(1)}, bf16[4,224,384]{2,1,0:T(8,128)(2,1)S(1)}, u32[]{:S(2)}, u32[]{:S(2)}) collective-permute-start(bf16[4,224,384]{2,1,0:T(8,128)(2,1)S(1)} %for_other.7), channel_id=1, source_target_pairs={{0,1},{1,0},{2,3},{3,2},{4,5},{5,4},{6,7},{7,6},{8,9},{9,8},{10,11... | collective-permute-start | bytes 2064392 | tf_op jit(solution)/shard_map/ppermute | solution.py:181
  103.5 0.7 collective-permute-start.26
  104.2 1.2 collective-permute-done.25.refs_1_.refs_8_.refs_7_
  105.4 0.7 for_other.8
  106.1 5.1 %collective-permute-start.27 = (bf16[2,224,384]{2,1,0:T(8,128)(2,1)S(1)}, bf16[2,224,384]{2,1,0:T(8,128)(2,1)S(1)}, u32[]{:S(2)}, u32[]{:S(2)}) collective-permute-start(bf16[2,224,384]{2,1,0:T(8,128)(2,1)S(1)} %for_other.8), channel_id=1, source_target_pairs={{0,1},{1,0},{2,3},{3,2},{4,5},{5,4},{6,7},{7,6},{8,9},{9,8},{10,11... | collective-permute-start | bytes 1032200 | tf_op jit(solution)/shard_map/ppermute | solution.py:181
  111.2 4.1 %down.4.refs_3_ = f32[448,1024]{1,0:T(8,128)S(1)} custom-call(s32[17]{0:T(128)S(1)} %dynamic-slice_bitcast_fusion.ids_ref.args_0_.refs_0_, bf16[224,6144]{1,0:T(8,128)(2,1)S(1)} %get-tuple-element.63.own_ref.args_4_.refs_4_, bf16[224,6144]{1,0:T(8,128)(2,1)S(1)} %collective-permute-done.16.other_ref, ...), custom_call_target="tpu_custom_call" | custom-call | flops 1000 | bytes 1000 | tf_op jit(solution)/shard_map/down/pallas_call | solution.py:242
  115.3 4.0 %act.5 = (bf16[224,6144]{1,0:T(8,128)(2,1)}, bf16[224,6144]{1,0:T(8,128)(2,1)}, f32[16,1,384]{2,1,0:T(1,128)S(1)}) custom-call(s32[17]{0:T(128)S(1)} %dynamic-slice_bitcast_fusion.ids_ref.args_0_.refs_0_, bf16[224,2048]{1,0:T(8,128)(2,1)} %bitcast.22, ...), custom_call_target="tpu_custom_call", output_to_operand_aliasing={{0}: (11, {}), {1}: (12, {})} | custom-call | flops 1000 | bytes 1000 | tf_op jit(solution)/shard_map/act/pallas_call | solution.py:317
  119.3 4.0 %act.6 = (bf16[224,6144]{1,0:T(8,128)(2,1)}, bf16[224,6144]{1,0:T(8,128)(2,1)}, f32[16,1,384]{2,1,0:T(1,128)S(1)}) custom-call(s32[17]{0:T(128)S(1)} %dynamic-slice_bitcast_fusion.ids_ref.args_0_.refs_0_, bf16[224,2048]{1,0:T(8,128)(2,1)} %bitcast.23, ...), custom_call_target="tpu_custom_call", output_to_operand_aliasing={{0}: (12, {}), {1}: (13, {})} | custom-call | flops 1000 | bytes 1000 | tf_op jit(solution)/shard_map/act/pallas_call | solution.py:317
  123.3 0.7 for_other.9
  124.0 0.1 collective-permute-start.28
  124.1 2.2 %down.5 = (bf16[224,1024]{1,0:T(8,128)(2,1)S(1)}, bf16[224,1024]{1,0:T(8,128)(2,1)S(1)}) custom-call(s32[17]{0:T(128)S(1)} %dynamic-slice_bitcast_fusion.ids_ref.args_0_.refs_0_, bf16[224,6144]{1,0:T(8,128)(2,1)S(1)} %get-tuple-element.63.own_ref.args_4_.refs_4_, bf16[224,6144]{1,0:T(8,128)(2,1)S(1)} %collective-permute-done.16.other_ref, ...), custom_call_target="tpu_custom_call" | custom-call | flops 2000000000 | bytes 1000 | tf_op jit(solution)/shard_map/down/pallas_call | solution.py:242
  126.3 0.0 copy-start.1
  126.3 3.6 %act.7 = (bf16[224,6144]{1,0:T(8,128)(2,1)}, bf16[224,6144]{1,0:T(8,128)(2,1)}, f32[16,1,384]{2,1,0:T(1,128)S(1)}) custom-call(s32[17]{0:T(128)S(1)} %dynamic-slice_bitcast_fusion.ids_ref.args_0_.refs_0_, bf16[224,2048]{1,0:T(8,128)(2,1)} %bitcast.24, ...), custom_call_target="tpu_custom_call", output_to_operand_aliasing={{0}: (10, {}), {1}: (11, {})} | custom-call | flops 1000 | bytes 1000 | tf_op jit(solution)/shard_map/act/pallas_call | solution.py:317
  129.9 0.6 collective-permute-start.29
  130.5 11.6 %all_to_all.17 = f32[16,1,384]{2,1,0:T(1,128)S(1)} all-to-all(f32[16,1,384]{2,1,0:T(1,128)S(1)} %get-tuple-element.84), channel_id=1, replica_groups=mesh['dp'=16,'expert'=8,'tensor'=2] {'dp'}, dimensions={0} | all-to-all | bytes 49152 | tf_op jit(solution)/shard_map/all_to_all | solution.py:473
  142.2 2.9 %all-gather.1 = f32[2,1,384]{2,1,0:T(1,128)S(1)} all-gather(f32[1,1,384]{2,1,0:T(1,128)S(1)} %reshape.21), channel_id=2, replica_groups=mesh['dp'=16,'expert'=8,'tensor'=2] {'tensor'}, dimensions={0}, use_global_device_ids=true | all-gather | bytes 4608 | tf_op jit(solution)/shard_map/all_gather | solution.py:474
  145.1 0.1 all_to_all.12
  145.2 10.7 %all_to_all.18 = f32[8,1,48]{2,1,0:T(1,128)S(1)} all-to-all(f32[8,1,48]{2,1,0:T(1,128)S(1)} %all_to_all.12), channel_id=1, replica_groups=mesh['dp'=16,'expert'=8,'tensor'=2] {'expert'}, dimensions={0} | all-to-all | bytes 3072 | tf_op jit(solution)/shard_map/all_to_all | solution.py:475
  155.9 0.7 unpack.1
  156.7 1.5 finish.1
  (43 shorter events, 0.2 us)
Async XLA Ops:
  1.3 0.7 copy-start.3
  3.5 0.6 copy-start
  4.2 14.1 %collective-permute-start = (bf16[48,1024]{1,0:T(8,128)(2,1)S(1)}, bf16[48,1024]{1,0:T(8,128)(2,1)S(1)}, u32[]{:S(2)}, u32[]{:S(2)}) collective-permute-start(bf16[48,1024]{1,0:T(8,128)(2,1)S(1)} %get-tuple-element.53), channel_id=1, source_target_pairs={{0,2},{2,4},{4,6},{6,8},{8,10},{10,12},{12,14},{14,0},{1,3},{3,5},... | collective-permute-start | bytes 294920 | tf_op jit(solution)/shard_map/ppermute | solution.py:408
  6.6 14.1 %collective-permute-start.1 = (bf16[48,1024]{1,0:T(8,128)(2,1)S(1)}, bf16[48,1024]{1,0:T(8,128)(2,1)S(1)}, u32[]{:S(2)}, u32[]{:S(2)}) collective-permute-start(bf16[48,1024]{1,0:T(8,128)(2,1)S(1)} %get-tuple-element.54), channel_id=1, source_target_pairs={{0,4},{2,6},{4,8},{6,10},{8,12},{10,14},{12,0},{14,2},{1,5},{3,7},... | collective-permute-start | bytes 294920 | tf_op jit(solution)/shard_map/ppermute | solution.py:408
  9.6 18.8 %collective-permute-start.2 = (bf16[48,1024]{1,0:T(8,128)(2,1)S(1)}, bf16[48,1024]{1,0:T(8,128)(2,1)S(1)}, u32[]{:S(2)}, u32[]{:S(2)}) collective-permute-start(bf16[48,1024]{1,0:T(8,128)(2,1)S(1)} %get-tuple-element.55), channel_id=1, source_target_pairs={{0,6},{2,8},{4,10},{6,12},{8,14},{10,0},{12,2},{14,4},{1,7},{3,9},... | collective-permute-start | bytes 294920 | tf_op jit(solution)/shard_map/ppermute | solution.py:408
  13.4 15.1 %collective-permute-start.3 = (bf16[48,1024]{1,0:T(8,128)(2,1)S(1)}, bf16[48,1024]{1,0:T(8,128)(2,1)S(1)}, u32[]{:S(2)}, u32[]{:S(2)}) collective-permute-start(bf16[48,1024]{1,0:T(8,128)(2,1)S(1)} %get-tuple-element.56), channel_id=1, source_target_pairs={{0,8},{2,10},{4,12},{6,14},{8,0},{10,2},{12,4},{14,6},{1,9},{3,11}... | collective-permute-start | bytes 294920 | tf_op jit(solution)/shard_map/ppermute | solution.py:408
  13.8 14.7 %collective-permute-start.4 = (bf16[48,1024]{1,0:T(8,128)(2,1)S(1)}, bf16[48,1024]{1,0:T(8,128)(2,1)S(1)}, u32[]{:S(2)}, u32[]{:S(2)}) collective-permute-start(bf16[48,1024]{1,0:T(8,128)(2,1)S(1)} %get-tuple-element.57), channel_id=1, source_target_pairs={{0,10},{2,12},{4,14},{6,0},{8,2},{10,4},{12,6},{14,8},{1,11},{3,13... | collective-permute-start | bytes 294920 | tf_op jit(solution)/shard_map/ppermute | solution.py:408
  18.3 10.1 %copy-start.4 = (bf16[48,1024]{1,0:T(8,128)(2,1)}, bf16[48,1024]{1,0:T(8,128)(2,1)S(1)}, u32[]{:S(2)}) copy-start(bf16[48,1024]{1,0:T(8,128)(2,1)S(1)} %collective-permute-done.refs_1_) | copy-start | bytes 294916
  18.3 14.9 %collective-permute-start.5 = (bf16[48,1024]{1,0:T(8,128)(2,1)S(1)}, bf16[48,1024]{1,0:T(8,128)(2,1)S(1)}, u32[]{:S(2)}, u32[]{:S(2)}) collective-permute-start(bf16[48,1024]{1,0:T(8,128)(2,1)S(1)} %get-tuple-element.58), channel_id=1, source_target_pairs={{0,12},{2,14},{4,0},{6,2},{8,4},{10,6},{12,8},{14,10},{1,13},{3,15... | collective-permute-start | bytes 294920 | tf_op jit(solution)/shard_map/ppermute | solution.py:408
  20.7 7.8 %copy-start.5 = (bf16[48,1024]{1,0:T(8,128)(2,1)}, bf16[48,1024]{1,0:T(8,128)(2,1)S(1)}, u32[]{:S(2)}) copy-start(bf16[48,1024]{1,0:T(8,128)(2,1)S(1)} %collective-permute-done.1.refs_2_) | copy-start | bytes 294916
  20.7 13.4 %collective-permute-start.6 = (bf16[48,1024]{1,0:T(8,128)(2,1)S(1)}, bf16[48,1024]{1,0:T(8,128)(2,1)S(1)}, u32[]{:S(2)}, u32[]{:S(2)}) collective-permute-start(bf16[48,1024]{1,0:T(8,128)(2,1)S(1)} %get-tuple-element.59), channel_id=1, source_target_pairs={{0,14},{2,0},{4,2},{6,4},{8,6},{10,8},{12,10},{14,12},{1,15},{3,1}... | collective-permute-start | bytes 294920 | tf_op jit(solution)/shard_map/ppermute | solution.py:408
  28.5 5.6 %copy-start.6 = (bf16[48,1024]{1,0:T(8,128)(2,1)}, bf16[48,1024]{1,0:T(8,128)(2,1)S(1)}, u32[]{:S(2)}) copy-start(bf16[48,1024]{1,0:T(8,128)(2,1)S(1)} %collective-permute-done.2.refs_3_) | copy-start | bytes 294916
  28.5 5.6 %copy-start.7 = (bf16[48,1024]{1,0:T(8,128)(2,1)}, bf16[48,1024]{1,0:T(8,128)(2,1)S(1)}, u32[]{:S(2)}) copy-start(bf16[48,1024]{1,0:T(8,128)(2,1)S(1)} %collective-permute-done.3.refs_4_) | copy-start | bytes 294916
  28.5 5.6 %copy-start.8 = (bf16[48,1024]{1,0:T(8,128)(2,1)}, bf16[48,1024]{1,0:T(8,128)(2,1)S(1)}, u32[]{:S(2)}) copy-start(bf16[48,1024]{1,0:T(8,128)(2,1)S(1)} %collective-permute-done.4.refs_5_) | copy-start | bytes 294916
  33.2 0.9 copy-start.9
  34.1 0.6 copy-start.10
  36.0 49.5 %collective-permute-start.16 = (bf16[224,6144]{1,0:T(8,128)(2,1)S(1)}, bf16[224,6144]{1,0:T(8,128)(2,1)S(1)}, u32[]{:S(2)}, u32[]{:S(2)}) collective-permute-start(bf16[224,6144]{1,0:T(8,128)(2,1)S(1)} %get-tuple-element.63.own_ref.args_4_.refs_4_), channel_id=1, source_target_pairs={{0,1},{1,0},{2,3},{3,2},{4,5},{5,4},{6,7},{7,6},{8,9},{9,8},{10,11... | collective-permute-start | bytes 8257544 | tf_op jit(solution)/shard_map/ppermute | solution.py:181
  36.7 15.8 %collective-permute-start.12 = (bf16[384,1024]{1,0:T(8,128)(2,1)S(1)}, bf16[384,1024]{1,0:T(8,128)(2,1)S(1)}, u32[]{:S(2)}, u32[]{:S(2)}) collective-permute-start(bf16[384,1024]{1,0:T(8,128)(2,1)S(1)} %in_order.1.refs_0_.args_5_), channel_id=1, source_target_pairs={{0,16},{1,65},{16,32},{17,81},{32,48},{33,97},{48,0},{49,113},{64,... | collective-permute-start | bytes 2359304 | tf_op jit(solution)/shard_map/ppermute | solution.py:177
  38.0 4.1 %collective-permute-start.11 = (bf16[224,1024]{1,0:T(8,128)(2,1)S(1)}, bf16[224,1024]{1,0:T(8,128)(2,1)S(1)}, u32[]{:S(2)}, u32[]{:S(2)}) collective-permute-start(bf16[224,1024]{1,0:T(8,128)(2,1)S(1)} %get-tuple-element.62), channel_id=1, source_target_pairs={{0,1},{1,0},{2,3},{3,2},{4,5},{5,4},{6,7},{7,6},{8,9},{9,8},{10,11... | collective-permute-start | bytes 1376264 | tf_op jit(solution)/shard_map/ppermute | solution.py:181
  38.3 17.7 %collective-permute-start.9 = (bf16[384,1024]{1,0:T(8,128)(2,1)S(1)}, bf16[384,1024]{1,0:T(8,128)(2,1)S(1)}, u32[]{:S(2)}, u32[]{:S(2)}) collective-permute-start(bf16[384,1024]{1,0:T(8,128)(2,1)S(1)} %in_order.1.refs_0_.args_5_), channel_id=1, source_target_pairs={{0,192},{1,49},{16,208},{17,1},{32,224},{33,17},{48,240},{49,33},{... | collective-permute-start | bytes 2359304 | tf_op jit(solution)/shard_map/ppermute | solution.py:177
  40.5 17.3 %collective-permute-start.8 = (bf16[384,1024]{1,0:T(8,128)(2,1)S(1)}, bf16[384,1024]{1,0:T(8,128)(2,1)S(1)}, u32[]{:S(2)}, u32[]{:S(2)}) collective-permute-start(bf16[384,1024]{1,0:T(8,128)(2,1)S(1)} %in_order.1.refs_0_.args_5_), channel_id=1, source_target_pairs={{0,64},{1,17},{16,80},{17,33},{32,96},{33,49},{48,112},{49,1},{64,... | collective-permute-start | bytes 2359304 | tf_op jit(solution)/shard_map/ppermute | solution.py:177
  42.1 16.9 %collective-permute-start.7 = (bf16[384,1024]{1,0:T(8,128)(2,1)S(1)}, bf16[384,1024]{1,0:T(8,128)(2,1)S(1)}, u32[]{:S(2)}, u32[]{:S(2)}) collective-permute-start(bf16[384,1024]{1,0:T(8,128)(2,1)S(1)} %in_order.1.refs_0_.args_5_), channel_id=1, source_target_pairs={{0,48},{1,193},{16,0},{17,209},{32,16},{33,225},{48,32},{49,241},{... | collective-permute-start | bytes 2359304 | tf_op jit(solution)/shard_map/ppermute | solution.py:177
  52.5 13.8 %collective-permute-start.15 = (bf16[384,1024]{1,0:T(8,128)(2,1)S(1)}, bf16[384,1024]{1,0:T(8,128)(2,1)S(1)}, u32[]{:S(2)}, u32[]{:S(2)}) collective-permute-start(bf16[384,1024]{1,0:T(8,128)(2,1)S(1)} %collective-permute-done.12.refs_1_.args_6_), channel_id=1, source_target_pairs={{0,192},{1,49},{16,208},{17,1},{32,224},{33,17},{48,240},{49,33},{... | collective-permute-start | bytes 2359304 | tf_op jit(solution)/shard_map/ppermute | solution.py:177
  56.0 17.1 %collective-permute-start.14 = (bf16[384,1024]{1,0:T(8,128)(2,1)S(1)}, bf16[384,1024]{1,0:T(8,128)(2,1)S(1)}, u32[]{:S(2)}, u32[]{:S(2)}) collective-permute-start(bf16[384,1024]{1,0:T(8,128)(2,1)S(1)} %collective-permute-done.12.refs_1_.args_6_), channel_id=1, source_target_pairs={{0,64},{1,17},{16,80},{17,33},{32,96},{33,49},{48,112},{49,1},{64,... | collective-permute-start | bytes 2359304 | tf_op jit(solution)/shard_map/ppermute | solution.py:177
  57.7 19.2 %collective-permute-start.13 = (bf16[384,1024]{1,0:T(8,128)(2,1)S(1)}, bf16[384,1024]{1,0:T(8,128)(2,1)S(1)}, u32[]{:S(2)}, u32[]{:S(2)}) collective-permute-start(bf16[384,1024]{1,0:T(8,128)(2,1)S(1)} %collective-permute-done.12.refs_1_.args_6_), channel_id=1, source_target_pairs={{0,16},{1,65},{16,32},{17,81},{32,48},{33,97},{48,0},{49,113},{64,... | collective-permute-start | bytes 2359304 | tf_op jit(solution)/shard_map/ppermute | solution.py:177
  60.5 19.2 %collective-permute-start.23 = (bf16[5,224,384]{2,1,0:T(8,128)(2,1)S(1)}, bf16[5,224,384]{2,1,0:T(8,128)(2,1)S(1)}, u32[]{:S(2)}, u32[]{:S(2)}) collective-permute-start(bf16[5,224,384]{2,1,0:T(8,128)(2,1)S(1)} %for_other.6), channel_id=1, source_target_pairs={{0,1},{1,0},{2,3},{3,2},{4,5},{5,4},{6,7},{7,6},{8,9},{9,8},{10,11... | collective-permute-start | bytes 2580488 | tf_op jit(solution)/shard_map/ppermute | solution.py:181
  66.3 18.9 %collective-permute-start.10 = (bf16[384,1024]{1,0:T(8,128)(2,1)S(1)}, bf16[384,1024]{1,0:T(8,128)(2,1)S(1)}, u32[]{:S(2)}, u32[]{:S(2)}) collective-permute-start(bf16[384,1024]{1,0:T(8,128)(2,1)S(1)} %collective-permute-done.7.refs_2_.args_7_), channel_id=1, source_target_pairs={{0,64},{1,17},{16,80},{17,33},{32,96},{33,49},{48,112},{49,1},{64,... | collective-permute-start | bytes 2359304 | tf_op jit(solution)/shard_map/ppermute | solution.py:177
  76.9 16.6 %collective-permute-start.17 = (bf16[384,1024]{1,0:T(8,128)(2,1)S(1)}, bf16[384,1024]{1,0:T(8,128)(2,1)S(1)}, u32[]{:S(2)}, u32[]{:S(2)}) collective-permute-start(bf16[384,1024]{1,0:T(8,128)(2,1)S(1)} %collective-permute-done.13.refs_0_.refs_5_.refs_4_), channel_id=1, source_target_pairs={{0,64},{1,17},{16,80},{17,33},{32,96},{33,49},{48,112},{49,1},{64,... | collective-permute-start | bytes 2359304 | tf_op jit(solution)/shard_map/ppermute | solution.py:177
  76.9 16.6 %collective-permute-start.19 = (bf16[384,1024]{1,0:T(8,128)(2,1)S(1)}, bf16[384,1024]{1,0:T(8,128)(2,1)S(1)}, u32[]{:S(2)}, u32[]{:S(2)}) collective-permute-start(bf16[384,1024]{1,0:T(8,128)(2,1)S(1)} %collective-permute-done.13.refs_0_.refs_5_.refs_4_), channel_id=1, source_target_pairs={{0,192},{1,49},{16,208},{17,1},{32,224},{33,17},{48,240},{49,33},{... | collective-permute-start | bytes 2359304 | tf_op jit(solution)/shard_map/ppermute | solution.py:177
  79.6 17.4 %collective-permute-start.21 = (bf16[384,1024]{1,0:T(8,128)(2,1)S(1)}, bf16[384,1024]{1,0:T(8,128)(2,1)S(1)}, u32[]{:S(2)}, u32[]{:S(2)}) collective-permute-start(bf16[384,1024]{1,0:T(8,128)(2,1)S(1)} %collective-permute-done.7.refs_2_.args_7_), channel_id=1, source_target_pairs={{0,192},{1,49},{16,208},{17,1},{32,224},{33,17},{48,240},{49,33},{... | collective-permute-start | bytes 2359304 | tf_op jit(solution)/shard_map/ppermute | solution.py:177
  85.2 18.3 %collective-permute-start.24 = (bf16[384,1024]{1,0:T(8,128)(2,1)S(1)}, bf16[384,1024]{1,0:T(8,128)(2,1)S(1)}, u32[]{:S(2)}, u32[]{:S(2)}) collective-permute-start(bf16[384,1024]{1,0:T(8,128)(2,1)S(1)} %collective-permute-done.8.refs_3_.args_8_), channel_id=1, source_target_pairs={{0,64},{1,17},{16,80},{17,33},{32,96},{33,49},{48,112},{49,1},{64,... | collective-permute-start | bytes 2359304 | tf_op jit(solution)/shard_map/ppermute | solution.py:177
  85.5 19.9 %collective-permute-start.25 = (bf16[384,1024]{1,0:T(8,128)(2,1)S(1)}, bf16[384,1024]{1,0:T(8,128)(2,1)S(1)}, u32[]{:S(2)}, u32[]{:S(2)}) collective-permute-start(bf16[384,1024]{1,0:T(8,128)(2,1)S(1)} %collective-permute-done.15.refs_2_.refs_6_.refs_1_), channel_id=1, source_target_pairs={{0,192},{1,49},{16,208},{17,1},{32,224},{33,17},{48,240},{49,33},{... | collective-permute-start | bytes 2359304 | tf_op jit(solution)/shard_map/ppermute | solution.py:177
  93.6 29.7 %collective-permute-start.18 = (bf16[384,1024]{1,0:T(8,128)(2,1)S(1)}, bf16[384,1024]{1,0:T(8,128)(2,1)S(1)}, u32[]{:S(2)}, u32[]{:S(2)}) collective-permute-start(bf16[384,1024]{1,0:T(8,128)(2,1)S(1)} %collective-permute-done.10.refs_0_.refs_7_.refs_2_), channel_id=1, source_target_pairs={{0,64},{1,17},{16,80},{17,33},{32,96},{33,49},{48,112},{49,1},{64,... | collective-permute-start | bytes 2359304 | tf_op jit(solution)/shard_map/ppermute | solution.py:177
  93.6 29.7 %collective-permute-start.20 = (bf16[384,1024]{1,0:T(8,128)(2,1)S(1)}, bf16[384,1024]{1,0:T(8,128)(2,1)S(1)}, u32[]{:S(2)}, u32[]{:S(2)}) collective-permute-start(bf16[384,1024]{1,0:T(8,128)(2,1)S(1)} %collective-permute-done.19.refs_3_.refs_6_.refs_1_), channel_id=1, source_target_pairs={{0,192},{1,49},{16,208},{17,1},{32,224},{33,17},{48,240},{49,33},{... | collective-permute-start | bytes 2359304 | tf_op jit(solution)/shard_map/ppermute | solution.py:177
  98.2 17.1 %collective-permute-start.22 = (bf16[4,224,384]{2,1,0:T(8,128)(2,1)S(1)}, bf16[4,224,384]{2,1,0:T(8,128)(2,1)S(1)}, u32[]{:S(2)}, u32[]{:S(2)}) collective-permute-start(bf16[4,224,384]{2,1,0:T(8,128)(2,1)S(1)} %for_other.7), channel_id=1, source_target_pairs={{0,1},{1,0},{2,3},{3,2},{4,5},{5,4},{6,7},{7,6},{8,9},{9,8},{10,11... | collective-permute-start | bytes 2064392 | tf_op jit(solution)/shard_map/ppermute | solution.py:181
  103.5 11.8 %collective-permute-start.26 = (bf16[3,224,384]{2,1,0:T(8,128)(2,1)S(1)}, bf16[3,224,384]{2,1,0:T(8,128)(2,1)S(1)}, u32[]{:S(2)}, u32[]{:S(2)}) collective-permute-start(bf16[3,224,384]{2,1,0:T(8,128)(2,1)S(1)} %for_other.5), channel_id=1, source_target_pairs={{0,1},{1,0},{2,3},{3,2},{4,5},{5,4},{6,7},{7,6},{8,9},{9,8},{10,11... | collective-permute-start | bytes 1548296 | tf_op jit(solution)/shard_map/ppermute | solution.py:181
  106.1 13.2 %collective-permute-start.27 = (bf16[2,224,384]{2,1,0:T(8,128)(2,1)S(1)}, bf16[2,224,384]{2,1,0:T(8,128)(2,1)S(1)}, u32[]{:S(2)}, u32[]{:S(2)}) collective-permute-start(bf16[2,224,384]{2,1,0:T(8,128)(2,1)S(1)} %for_other.8), channel_id=1, source_target_pairs={{0,1},{1,0},{2,3},{3,2},{4,5},{5,4},{6,7},{7,6},{8,9},{9,8},{10,11... | collective-permute-start | bytes 1032200 | tf_op jit(solution)/shard_map/ppermute | solution.py:181
  124.0 2.3 %collective-permute-start.28 = (bf16[2,224,384]{2,1,0:T(8,128)(2,1)S(1)}, bf16[2,224,384]{2,1,0:T(8,128)(2,1)S(1)}, u32[]{:S(2)}, u32[]{:S(2)}) collective-permute-start(bf16[2,224,384]{2,1,0:T(8,128)(2,1)S(1)} %for_other.9), channel_id=1, source_target_pairs={{0,1},{1,0},{2,3},{3,2},{4,5},{5,4},{6,7},{7,6},{8,9},{9,8},{10,11... | collective-permute-start | bytes 1032200 | tf_op jit(solution)/shard_map/ppermute | solution.py:181
  126.3 29.6 %copy-start.1 = (s32[128,2]{0,1:T(2,128)S(1)}, s32[128,2]{0,1:T(2,128)}, u32[]{:S(2)}) copy-start(s32[128,2]{0,1:T(2,128)} %param.12) | copy-start | bytes 3076
  126.3 29.6 %copy-start.2 = (bf16[128,2]{0,1:T(2,128)(2,1)S(1)}, bf16[128,2]{0,1:T(2,128)(2,1)}, u32[]{:S(2)}) copy-start(bf16[128,2]{0,1:T(2,128)(2,1)} %param.13) | copy-start | bytes 1540
  129.9 26.7 %collective-permute-start.29 = (bf16[224,1024]{1,0:T(8,128)(2,1)S(1)}, bf16[224,1024]{1,0:T(8,128)(2,1)S(1)}, u32[]{:S(2)}, u32[]{:S(2)}) collective-permute-start(bf16[224,1024]{1,0:T(8,128)(2,1)S(1)} %get-tuple-element.85), channel_id=1, source_target_pairs={{0,1},{1,0},{2,3},{3,2},{4,5},{5,4},{6,7},{7,6},{8,9},{9,8},{10,11... | collective-permute-start | bytes 1376264 | tf_op jit(solution)/shard_map/ppermute | solution.py:181
where the time goes:
time: 159 us; the launch traced here: 158 us
  starting transfers between devices  52.2 us (33%)
  Pallas kernels  42.2 us (27%)
  waiting for transfers between devices  34.8 us (22%)
  blocking collectives  25.3 us (16%)
  local copies, waits for them, and re-layouts  2.73 us (2%)
    ppermute x15, waiting for transfers between devices, hop(): return lax.ppermute(array, ('dp', 'tensor'), shifts(first, second))  27.6 us
    ppermute x15, starting transfers between devices, hop(): return lax.ppermute(array, ('dp', 'tensor'), shifts(first, second))  20.3 us
    ppermute x7, starting transfers between devices, local(): lax.ppermute(sent[k], 'expert', [(i, (i + k) % experts) for i in range(ex...  17.3 us
    pallas_call x4, Pallas kernels, act(): pl.pallas_call(functools.partial(act_kernel_first if first else act_kerne...  15.9 us
    ppermute x8, starting transfers between devices, swap(): return lax.ppermute(array, 'tensor', [(0, 1), (1, 0)])  14.7 us
    all_to_all x1, blocking collectives, local(): lax.all_to_all(probe.reshape(columns, rows), 'dp', 0, 0, tiled=True)  11.6 us
    all_to_all x1, blocking collectives, local(): lax.all_to_all(totals.reshape(experts, cap), 'expert', 0, 0, tiled=True)  10.7 us
    pallas_call x3, Pallas kernels, down(): pl.pallas_call(functools.partial(down_kernel, n, start, first, last), in_...  9.26 us
  transfers between devices with their start and end apart: 30, of which 12 were waited for; matrix products, arithmetic and copies ran while one was open for 0% of the time, Pallas kernels for 21%

commit v1 on v0

--- a/solution.py
+++ b/solution.py
@@ -105,39 +105,63 @@
     )(table, ids, pos, probs)
 
 
-def prepare_kernel(ids_ref, gate_ref, up_ref, w_ref, slope_ref, act_ref, hidden_ref, half_ref):
+def prepare_kernel(ids_ref, gate_ref, up_ref, w_ref, slope_ref, act_ref, give_ref, keep_ref):
+    core = ids_ref[ids_ref.shape[0] - 1]
+    slots, width = gate_ref.shape[1], keep_ref.shape[1]
     gate = gate_ref[...].astype(jnp.float32)
     up = up_ref[...].astype(jnp.float32)
     logistic = 1.0 / (1.0 + jnp.exp(-gate))
     activated = gate * logistic
     slope_ref[...] = (up * logistic * (1.0 + gate * (1.0 - logistic))).astype(jnp.bfloat16)
     act_ref[...] = activated.astype(jnp.bfloat16)
-    hidden_ref[...] = (activated * up).astype(jnp.bfloat16)
-    half_ref[...] = w_ref[...]
+    give_ref[:, :slots] = (activated * up).astype(jnp.bfloat16)
+    give_ref[:, slots:] = w_ref[:, pl.ds(pl.multiple_of((1 - core) * width, 128), width)]
+    keep_ref[...] = w_ref[:, pl.ds(pl.multiple_of(core * width, 128), width)]
 
 
 def prepare(ids, gate, up, weight):
     f, slots = gate.shape
     width = weight.shape[1] // 2
     step = 32
-    columns = ids.shape[0] - 1
-    spec = pl.BlockSpec((step, slots), lambda i, ids: (i, 0))
+
+    def rows_of(columns):
+        return pl.BlockSpec((step, columns), lambda i, ids: (i, 0))
+
     return pl.pallas_call(
         prepare_kernel,
         grid_spec=pltpu.PrefetchScalarGridSpec(
             num_scalar_prefetch=1,
             grid=(f // step,),
-            in_specs=[
-                spec, spec, pl.BlockSpec((step, width), lambda i, ids: (i, 1 - ids[columns]))
-            ],
-            out_specs=[spec] * 3 + [pl.BlockSpec((step, width), lambda i, ids: (i, 0))],
+            in_specs=[rows_of(slots), rows_of(slots), rows_of(2 * width)],
+            out_specs=[rows_of(slots), rows_of(slots), rows_of(slots + width), rows_of(width)],
         ),
-        out_shape=[jax.ShapeDtypeStruct(gate.shape, jnp.bfloat16)] * 3
-        + [jax.ShapeDtypeStruct((f, width), jnp.bfloat16)],
+        out_shape=[
+            jax.ShapeDtypeStruct((f, columns), jnp.bfloat16)
+            for columns in (slots, slots, slots + width, width)
+        ],
         compiler_params=params(10),
         cost_estimate=cost(4000 * 1000 * 1000, 10 * f * slots),
         name="prepare",
     )(ids, gate, up, weight)
+
+
+def join_kernel(a_ref, b_ref, out_ref):
+    rows = a_ref.shape[0]
+    out_ref[:rows] = a_ref[...]
+    out_ref[rows:] = b_ref[...]
+
+
+def join(a, b):
+    rows, width = a.shape
+    return pl.pallas_call(
+        join_kernel,
+        in_specs=[VMEM, VMEM],
+        out_specs=VMEM,
+        out_shape=jax.ShapeDtypeStruct((2 * rows, width), a.dtype),
+        compiler_params=params(),
+        cost_estimate=cost(),
+        name="join",
+    )(a, b)
 
 
 def order_kernel(e_ref, *refs):
@@ -181,35 +205,45 @@
     return lax.ppermute(array, "tensor", [(0, 1), (1, 0)])
 
 
-def other_kernel(w_ref, *refs):
-    *blocks, out = refs
-    for i, block in enumerate(blocks):
+def distinct(blocks):
+    arrays, at = [], []
+    for array, row in blocks:
+        if not any(array is other for other in arrays):
+            arrays.append(array)
+        at.append(([array is other for other in arrays].index(True), row))
+    return arrays, at
+
+
+def other_kernel(at, rows, give_ref, *refs):
+    *arrays, out = refs
+    width = arrays[0].shape[1]
+    weight = give_ref[:, give_ref.shape[1] - width :]
+    for i, (which, row) in enumerate(at):
         out[i] = lax.dot_general(
-            w_ref[...], block[...], NT, preferred_element_type=jnp.float32
+            weight, arrays[which][row : row + rows], NT, preferred_element_type=jnp.float32
         ).astype(jnp.bfloat16)
 
 
-def for_other(weight, blocks):
-    f, width = weight.shape
-    rows = blocks[0].shape[0]
-    n = len(blocks)
-    return pl.pallas_call(
-        other_kernel,
-        in_specs=[VMEM] * (n + 1),
+def for_other(given, rows, blocks):
+    f = given.shape[0]
+    arrays, at = distinct(blocks)
+    return pl.pallas_call(
+        functools.partial(other_kernel, at, rows),
+        in_specs=[VMEM] * (1 + len(arrays)),
         out_specs=VMEM,
-        out_shape=jax.ShapeDtypeStruct((n, f, rows), jnp.bfloat16),
+        out_shape=jax.ShapeDtypeStruct((len(at), f, rows), jnp.bfloat16),
         compiler_params=params(10),
         cost_estimate=cost(),
         name="for_other",
-    )(weight, *blocks)
-
-
-def down_kernel(n, start, first, last, ids_ref, own_ref, other_ref, *refs):
-    blocks, refs = refs[:n], refs[n:]
+    )(in_vmem(given), *arrays)
+
+
+def down_kernel(at, n, rows, start, first, last, ids_ref, own_ref, other_ref, *refs):
+    arrays, refs = refs[:n], refs[n:]
     both = refs[-1]
     f = own_ref.shape[0]
-    rows, width = blocks[0].shape
-    for j in range(n):
+    width = arrays[0].shape[1]
+    for j in range(len(at)):
         column = pl.ds(pl.multiple_of(ids_ref[start + j] * rows, 128), rows)
         both[:f, j * rows : (j + 1) * rows] = own_ref[:, column]
         both[f:, j * rows : (j + 1) * rows] = other_ref[:, column]
@@ -220,7 +254,7 @@
         part = pl.ds(pl.multiple_of(t * tile, tile), tile)
         total = jnp.dot(
             both[...],
-            jnp.concatenate([block[:, part] for block in blocks], axis=0),
+            jnp.concatenate([arrays[w][row : row + rows, part] for w, row in at], axis=0),
             preferred_element_type=jnp.float32,
         )
         if not first:
@@ -233,22 +267,22 @@
             refs[1 - first][:, part] = total
 
 
-def down(ids, start, own, other, blocks, acc, last):
+def down(ids, start, own, other, rows, blocks, acc, last):
     f = own.shape[0]
-    rows, width = blocks[0].shape
-    n = len(blocks)
+    arrays, at = distinct(blocks)
+    n, width = len(arrays), arrays[0].shape[1]
     first = acc is None
     half = jax.ShapeDtypeStruct((f, width), jnp.bfloat16)
     return pl.pallas_call(
-        functools.partial(down_kernel, n, start, first, last),
+        functools.partial(down_kernel, at, n, rows, start, first, last),
         in_specs=[SMEM] + [VMEM] * (2 + n + (not first)),
         out_specs=[VMEM, VMEM] if last else VMEM,
         out_shape=[half, half] if last else jax.ShapeDtypeStruct((2 * f, width), jnp.float32),
-        scratch_shapes=[pltpu.VMEM((2 * f, n * rows), jnp.bfloat16)],
+        scratch_shapes=[pltpu.VMEM((2 * f, len(at) * rows), jnp.bfloat16)],
         compiler_params=params(16),
         cost_estimate=cost(2000 * 1000 * 1000, 1000) if last else cost(),
         name="down",
-    )(ids, in_vmem(own), in_vmem(other), *blocks, *([] if first else [acc]))
+    )(ids, in_vmem(own), in_vmem(other), *arrays, *([] if first else [acc]))
 
 
 def finish_kernel(ids_ref, mine_ref, theirs_ref, out_ref):
@@ -271,52 +305,44 @@
     )(ids, mine, theirs)
 
 
-def act_kernel(n, start, where, groups, ids_ref, w_ref, slope_ref, act_ref, hidden_ref, *refs):
-    blocks, parts = refs[:n], refs[n : n + groups]
-    gate_out, up_out, probe_out, gate_buf, up_buf, weight, sems = refs[-7:]
-    rows, width = blocks[0].shape
-    core = ids_ref[ids_ref.shape[0] - 1]
-    load = pltpu.make_async_copy(
-        w_ref.at[:, pl.ds(pl.multiple_of(core * width, 128), width)], weight, sems.at[2, 0]
-    )
-    load.start()
-    load.wait()
-
-    def copies(j):
+def act_kernel(at, n, rows, start, where, groups, ids_ref, *refs):
+    weight, slope_ref, act_ref, hidden_ref = refs[:4]
+    arrays, parts = refs[4 : 4 + n], refs[4 + n : 4 + n + groups]
+    refs = refs[4 + n + groups :]
+    gate_out, up_out, probe_out, gate_buf, up_buf, sems = refs[-6:]
+    if len(refs) > 6:
+        probe_out[...] = refs[2][...]
+    copies = []
+    for j, (which, row) in enumerate(at):
         column = pl.ds(pl.multiple_of(ids_ref[start + j] * rows, 128), rows)
-        return (
+        group, i = where[j]
+        upstream = lax.dot_general(
+            weight[...], arrays[which][row : row + rows], NT, preferred_element_type=jnp.float32
+        ) + parts[group][i].astype(jnp.float32)
+        gate_buf[j] = (upstream * slope_ref[:, column].astype(jnp.float32)).astype(jnp.bfloat16)
+        up_buf[j] = (upstream * act_ref[:, column].astype(jnp.float32)).astype(jnp.bfloat16)
+        copies += [
             pltpu.make_async_copy(gate_buf.at[j], gate_out.at[:, column], sems.at[0, j]),
             pltpu.make_async_copy(up_buf.at[j], up_out.at[:, column], sems.at[1, j]),
-        )
-
-    for j in range(n):
-        upstream = lax.dot_general(
-            weight[...], blocks[j][...], NT, preferred_element_type=jnp.float32
-        )
-        group, at = where[j]
-        upstream = upstream + parts[group][at].astype(jnp.float32)
-        column = pl.ds(pl.multiple_of(ids_ref[start + j] * rows, 128), rows)
-        gate_buf[j] = (upstream * slope_ref[:, column].astype(jnp.float32)).astype(jnp.bfloat16)
-        up_buf[j] = (upstream * act_ref[:, column].astype(jnp.float32)).astype(jnp.bfloat16)
-        for copy in copies(j):
+        ]
+        for copy in copies[-2:]:
             copy.start()
         probe_out[ids_ref[start + j]] = jnp.sum(
             upstream * hidden_ref[:, column].astype(jnp.float32), axis=0, keepdims=True
         )
-    for j in range(n):
-        for copy in copies(j):
-            copy.wait()
-
-
-def act(ids, start, weight, slope, activated, hidden, blocks, parts, where, held):
+    for copy in copies:
+        copy.wait()
+
+
+def act(ids, start, weight, slope, activated, hidden, rows, blocks, parts, where, held):
     f, slots = slope.shape
-    rows = blocks[0].shape[0]
-    n, groups = len(blocks), len(parts)
+    arrays, at = distinct(blocks)
+    n, groups = len(arrays), len(parts)
     first = held is None
     base = 5 + n + groups
     return pl.pallas_call(
-        functools.partial(act_kernel_first if first else act_kernel_next, n, start, where, groups),
-        in_specs=[SMEM, ANY] + [VMEM] * (3 + n + groups) + ([] if first else [ANY, ANY, VMEM]),
+        functools.partial(act_kernel, at, n, rows, start, where, groups),
+        in_specs=[SMEM] + [VMEM] * (4 + n + groups) + ([] if first else [ANY, ANY, VMEM]),
         out_specs=[ANY, ANY, VMEM],
         out_shape=[
             jax.ShapeDtypeStruct((f, slots), jnp.bfloat16),
@@ -324,27 +350,18 @@
             jax.ShapeDtypeStruct((slots // rows, 1, rows), jnp.float32),
         ],
         scratch_shapes=[
-            pltpu.VMEM((n, f, rows), jnp.bfloat16),
-            pltpu.VMEM((n, f, rows), jnp.bfloat16),
-            pltpu.VMEM((f, blocks[0].shape[1]), jnp.bfloat16),
-            pltpu.SemaphoreType.DMA((3, n)),
+            pltpu.VMEM((len(at), f, rows), jnp.bfloat16),
+            pltpu.VMEM((len(at), f, rows), jnp.bfloat16),
+            pltpu.SemaphoreType.DMA((2, len(at))),
         ],
         input_output_aliases={} if first else {base: 0, base + 1: 1},
         compiler_params=params(16),
         cost_estimate=cost(),
         name="act",
-    )(ids, in_hbm(weight), in_vmem(slope), in_vmem(activated), in_vmem(hidden), *blocks, *parts, *([] if first else held))
-
-
-def act_kernel_first(*args):
-    act_kernel(*args)
-
-
-def act_kernel_next(n, start, where, groups, *refs):
-    inputs = refs[: 5 + n + groups]
-    held_probe, probe_out = refs[5 + n + groups + 2], refs[-5]
-    probe_out[...] = held_probe[...]
-    act_kernel(n, start, where, groups, *inputs, *refs[-7:])
+    )(
+        ids, in_vmem(weight), in_vmem(slope), in_vmem(activated), in_vmem(hidden), *arrays,
+        *parts, *([] if first else held),
+    )
 
 
 def in_hbm(array):
@@ -361,17 +378,10 @@
 
 ACT = (
     ((0, 0), (1, 0), (-1, 0), (0, 1), (0, -1)),
-    ((1, 1), (1, -1), (-1, 1), (-1, -1)),
-    ((2, 0), (0, 2), (2, 1), (1, 2)),
-    ((-1, 2), (2, -1), (2, 2)),
+    ((2, 0), (0, 2), (1, 1), (-1, 1), (1, -1), (-1, -1)),
+    ((2, 1), (2, -1), (1, 2), (-1, 2), (2, 2)),
 )
-OTHER = (
-    ((0, 0), (1, 0), (-1, 0), (0, 1), (0, -1)),
-    ((2, 0), (1, 1), (1, -1)),
-    ((-1, 1), (-1, -1), (2, 1), (2, -1)),
-    ((0, 2), (1, 2)),
-    ((-1, 2), (2, 2)),
-)
+OTHER = (ACT[0], ACT[1], ((2, 1), (2, -1), (2, 2)), ((1, 2), (-1, 2)))
 LABELS = sum(ACT, ())
 PLACE = {label: (g, i) for g, labels in enumerate(OTHER) for i, label in enumerate(labels)}
 
@@ -404,22 +414,32 @@
         after(e_arr, ids), in_hbm(out_grad), in_hbm(seq_ids), seq_weights, in_hbm(expert_ids.T),
         in_hbm(route_probs.T), experts, cap
     )
-    chunks = [sent[0]] + [
-        lax.ppermute(sent[k], "expert", [(i, (i + k) % experts) for i in range(experts)])
-        for k in range(1, experts)
-    ]
-    slope, activated, hidden, w_send = prepare(
+    arrived = {0: sent[0]}
+    half_way = experts // 2
+    nearest = (1, experts - 1)
+    middle = [k for k in range(2, experts - 1) if abs(k - half_way) > 1]
+    for k in nearest + (half_way + 1, half_way, half_way - 1) + tuple(middle):
+        chunk = sent[k]
+        if k in middle:
+            chunk = after(chunk, arrived[nearest[k < half_way]])
+        arrived[k] = lax.ppermute(
+            chunk, "expert", [(i, (i + k) % experts) for i in range(experts)]
+        )
+    chunks = [arrived[k] for k in range(experts)]
+    slope, activated, give, w_own = prepare(
         ids, in_hbm(gate_pre[0]), in_hbm(after(up_pre[0], pos)), in_hbm(weight)
     )
-    block = in_order(after(e_arr, hidden), [in_hbm(c) for c in chunks])
-    w_other = swap(after(w_send, block))
-    hidden_other = swap(after(hidden, block))
-
-    b = {(0, 0): block}
+    block = in_order(after(e_arr, give), [in_hbm(c) for c in chunks])
+    got = swap(after(give, block))
+
+    b = {(0, 0): (block, 0)}
     parts, held = [], None
 
-    def other():
-        parts.append(swap(for_other(w_other, [b[l] for l in OTHER[len(parts)]])))
+    def share(step, *others):
+        blocks = [b[l] for l in OTHER[step]]
+        raw = for_other(after(got, *others) if others else got, rows, blocks)
+        parts.append(swap(raw))
+        return raw
 
     def activate(step, held):
         labels = ACT[step]
@@ -427,47 +447,41 @@
         where = [(need.index(PLACE[s, f][0]), PLACE[s, f][1]) for f, s in labels]
         start = sum(len(a) for a in ACT[:step])
         return act(
-            ids, start, weight, slope, activated, hidden, [b[l] for l in labels],
+            ids, start, w_own, slope, activated, give, rows, [b[l] for l in labels],
             [parts[g] for g in need], where, held,
         )
 
-    def send_both(first, source):
-        b[first, 1] = hop(source, 0, 1)
-        b[first, -1] = hop(source, 0, -1)
-
-    b[1, 0] = hop(block, 1, 0)
-    b[-1, 0] = hop(block, -1, 0)
-    send_both(0, block)
-    b[2, 0] = hop(b[1, 0], 1, 0)
-    send_both(1, b[1, 0])
-    send_both(-1, after(b[-1, 0], b[0, 1], b[0, -1]))
-    raw = for_other(w_other, [b[l] for l in OTHER[0]])
-    parts.append(swap(raw))
-    send_both(2, after(b[2, 0], raw, b[1, 1], b[1, -1]))
+    def accumulate(step, acc, *others):
+        blocks = [b[l] for l in ACT[step]]
+        start = sum(len(a) for a in ACT[:step])
+        own = after(give, *others) if others else give
+        return down(ids, start, own, got, rows, blocks, acc, step == len(ACT) - 1)
+
+    right, left = hop(block, 1, 0), hop(block, -1, 0)
+    up_one, down_one = hop(block, 0, 1), hop(block, 0, -1)
+    b[1, 0], b[-1, 0], b[0, 1], b[0, -1] = (right, 0), (left, 0), (up_one, 0), (down_one, 0)
+    far = hop(right, 1, 0)
+    b[2, 0] = (far, 0)
+    pair = join(right, left)
+    pair_up, pair_down = hop(pair, 0, 1), hop(pair, 0, -1)
+    b[1, 1], b[-1, 1] = (pair_up, 0), (pair_up, rows)
+    b[1, -1], b[-1, -1] = (pair_down, 0), (pair_down, rows)
+    b[0, 2] = (hop(down_one, 0, -1), 0)
+    raw = share(0)
+    far_up, far_down = hop(after(far, raw), 0, 1), hop(after(far, raw), 0, -1)
+    b[2, 1], b[2, -1] = (far_up, 0), (far_down, 0)
     held = activate(0, held)
-    b[0, 2] = hop(after(b[0, 1], b[-1, 1], held[2]), 0, 1)
-    b[1, 2] = hop(after(b[1, -1], b[-1, 1], held[2]), 0, -1)
-    raw = for_other(w_other, [b[l] for l in OTHER[1]])
-    parts.append(swap(raw))
-    acc = down(ids, 0, hidden, hidden_other, [b[l] for l in ACT[0]], None, False)
-    b[-1, 2] = hop(after(b[-1, 1], raw, acc, b[2, 1]), 0, 1)
-    b[2, 2] = hop(after(b[2, -1], raw, acc, b[2, 1]), 0, -1)
-    raw = for_other(w_other, [b[l] for l in OTHER[2]])
-    parts.append(swap(raw))
+    acc = accumulate(0, None)
+    pair_far = hop(after(pair_up, held[2], acc, far_up), 0, 1)
+    b[1, 2], b[-1, 2] = (pair_far, 0), (pair_far, rows)
+    b[2, 2] = (hop(far_down, 0, -1), 0)
+    share(1)
     held = activate(1, held)
-    raw = for_other(w_other, [b[l] for l in OTHER[3]])
-    parts.append(swap(raw))
-    held = activate(2, held)
-    middle = ACT[1] + ACT[2]
-    acc = down(ids, len(ACT[0]), hidden, hidden_other, [b[l] for l in middle], acc, False)
-    last = after(b[-1, 2], held[2], acc)
-    raw = for_other(w_other, [last, b[2, 2]])
-    parts.append(swap(raw))
-    blocks = [after(b[ACT[3][0]], raw)] + [b[l] for l in ACT[3][1:]]
-    mine, theirs = down(
-        ids, len(ACT[0] + middle), hidden, hidden_other, blocks, acc, True
-    )
-    gate_out, up_out, probe = activate(3, held)
+    acc = accumulate(1, acc)
+    share(2, held[2], acc)
+    raw = share(3, parts[2])
+    mine, theirs = accumulate(2, acc, raw)
+    gate_out, up_out, probe = activate(2, held)
     grad_down = finish(ids, mine, swap(after(theirs, probe)))
 
     shared = jnp.sum(lax.all_to_all(probe.reshape(columns, rows), "dp", 0, 0, tiled=True), axis=0)

time: 159 us -> 149 us (0.937)
  starting transfers between devices: 52.2 us -> 43.7 us
  Pallas kernels: 42.2 us -> 36.5 us
  waiting for transfers between devices: 34.8 us -> 37.7 us
  blocking collectives: 25.3 us -> 27.3 us
    ppermute x8 -> x6, starting transfers between devices: 14.7 us -> 7.82 us  [swap(): return lax.ppermute(array, 'tensor', [(0, 1), (1, 0)])]
    ppermute x15 -> x12, waiting for transfers between devices: 27.6 us -> 33.9 us  [hop(): return lax.ppermute(array, ('dp', 'tensor'), shifts(first, second))]
    pallas_call x12 -> x11, Pallas kernels: 30.1 us -> 24.4 us  [the longest x3 10.4 us: act(): pl.pallas_call(functools.partial(act_kernel, at, n, rows, start, where, g...]
    ppermute x7, waiting for transfers between devices: 5.58 us -> 2.26 us  [local(): lax.ppermute(chunk, 'expert', [(i, (i + k) % experts) for i in range(expe...]
    ppermute x15 -> x12, starting transfers between devices: 20.3 us -> 18.6 us  [hop(): return lax.ppermute(array, ('dp', 'tensor'), shifts(first, second))]
  transfers between devices with their start and end apart: 30 -> 25, of which waited for: 12 -> 10; matrix products, arithmetic and copies ran while one was open for 0% -> 0% of each run, Pallas kernels for 21% -> 19%
where the time goes in v1:
time: 149 us
  starting transfers between devices  43.7 us (29%)
  waiting for transfers between devices  37.7 us (25%)
  Pallas kernels  36.5 us (24%)
  blocking collectives  27.3 us (18%)
  local copies, waits for them, and re-layouts  2.76 us (2%)
    ppermute x12, waiting for transfers between devices, hop(): return lax.ppermute(array, ('dp', 'tensor'), shifts(first, second))  33.9 us
    ppermute x12, starting transfers between devices, hop(): return lax.ppermute(array, ('dp', 'tensor'), shifts(first, second))  18.6 us
    ppermute x7, starting transfers between devices, local(): lax.ppermute(chunk, 'expert', [(i, (i + k) % experts) for i in range(expe...  17.2 us
    all_to_all x1, blocking collectives, local(): lax.all_to_all(probe.reshape(columns, rows), 'dp', 0, 0, tiled=True)  13.1 us
    all_to_all x1, blocking collectives, local(): lax.all_to_all(totals.reshape(experts, cap), 'expert', 0, 0, tiled=True)  11 us
    pallas_call x3, Pallas kernels, act(): pl.pallas_call(functools.partial(act_kernel, at, n, rows, start, where, g...  10.4 us
    pallas_call x3, Pallas kernels, down(): pl.pallas_call(functools.partial(down_kernel, at, n, rows, start, first,...  9.09 us
    ppermute x6, starting transfers between devices, swap(): return lax.ppermute(array, 'tensor', [(0, 1), (1, 0)])  7.82 us
  transfers between devices with their start and end apart: 25, of which 10 were waited for; matrix products, arithmetic and copies ran while one was open for 0% of the time, Pallas kernels for 19%

profile of v1, /device:TPU:1, one launch (start us, length us, event | category | flops | bytes accessed | tf_op | source)
XLA Modules:
  0.0 148.9 jit_solution(12016326402624153388)
XLA Ops:
  0.6 0.7 dynamic-slice_bitcast_fusion.ids_ref
  1.3 0.7 copy-done.3
  2.0 1.5 %pack.1 = (bf16[48,1024]{1,0:T(8,128)(2,1)S(1)}, bf16[48,1024]{1,0:T(8,128)(2,1)S(1)}, bf16[48,1024]{1,0:T(8,128)(2,1)S(1)}, bf16[48,1024]{1,0:T(8,128)(2,1)S(1)...) custom-call(s32[1]{0:T(128)} %bitcast.3.z_ref.e_ref, ...), custom_call_target="tpu_custom_call" | custom-call | flops 1000 | bytes 1000 | tf_op jit(solution)/shard_map/pack/pallas_call | solution.py:68
  3.5 0.0 copy-start
  3.5 0.6 copy-done
  4.2 2.5 %collective-permute-start = (bf16[48,1024]{1,0:T(8,128)(2,1)S(1)}, bf16[48,1024]{1,0:T(8,128)(2,1)S(1)}, u32[]{:S(2)}, u32[]{:S(2)}) collective-permute-start(bf16[48,1024]{1,0:T(8,128)(2,1)S(1)} %get-tuple-element.49), channel_id=1, source_target_pairs={{0,2},{2,4},{4,6},{6,8},{8,10},{10,12},{12,14},{14,0},{1,3},{3,5},... | collective-permute-start | bytes 294920 | tf_op jit(solution)/shard_map/ppermute | solution.py:425
  6.6 3.9 %collective-permute-start.1 = (bf16[48,1024]{1,0:T(8,128)(2,1)S(1)}, bf16[48,1024]{1,0:T(8,128)(2,1)S(1)}, u32[]{:S(2)}, u32[]{:S(2)}) collective-permute-start(bf16[48,1024]{1,0:T(8,128)(2,1)S(1)} %get-tuple-element.51), channel_id=1, source_target_pairs={{0,14},{2,0},{4,2},{6,4},{8,6},{10,8},{12,10},{14,12},{1,15},{3,1}... | collective-permute-start | bytes 294920 | tf_op jit(solution)/shard_map/ppermute | solution.py:425
  10.6 1.6 %collective-permute-start.3 = (bf16[48,1024]{1,0:T(8,128)(2,1)S(1)}, bf16[48,1024]{1,0:T(8,128)(2,1)S(1)}, u32[]{:S(2)}, u32[]{:S(2)}) collective-permute-start(bf16[48,1024]{1,0:T(8,128)(2,1)S(1)} %get-tuple-element.53), channel_id=1, source_target_pairs={{0,6},{2,8},{4,10},{6,12},{8,14},{10,0},{12,2},{14,4},{1,7},{3,9},... | collective-permute-start | bytes 294920 | tf_op jit(solution)/shard_map/ppermute | solution.py:425
  12.2 2.8 %collective-permute-start.4 = (bf16[48,1024]{1,0:T(8,128)(2,1)S(1)}, bf16[48,1024]{1,0:T(8,128)(2,1)S(1)}, u32[]{:S(2)}, u32[]{:S(2)}) collective-permute-start(bf16[48,1024]{1,0:T(8,128)(2,1)S(1)} %get-tuple-element.54), channel_id=1, source_target_pairs={{0,8},{2,10},{4,12},{6,14},{8,0},{10,2},{12,4},{14,6},{1,9},{3,11}... | collective-permute-start | bytes 294920 | tf_op jit(solution)/shard_map/ppermute | solution.py:425
  15.0 4.0 %collective-permute-start.5 = (bf16[48,1024]{1,0:T(8,128)(2,1)S(1)}, bf16[48,1024]{1,0:T(8,128)(2,1)S(1)}, u32[]{:S(2)}, u32[]{:S(2)}) collective-permute-start(bf16[48,1024]{1,0:T(8,128)(2,1)S(1)} %get-tuple-element.55), channel_id=1, source_target_pairs={{0,10},{2,12},{4,14},{6,0},{8,2},{10,4},{12,6},{14,8},{1,11},{3,13... | collective-permute-start | bytes 294920 | tf_op jit(solution)/shard_map/ppermute | solution.py:425
  19.1 0.0 collective-permute-done.refs_1_
  19.1 0.0 collective-permute-start.6
  19.1 2.3 %collective-permute-start.2 = (bf16[48,1024]{1,0:T(8,128)(2,1)S(1)}, bf16[48,1024]{1,0:T(8,128)(2,1)S(1)}, u32[]{:S(2)}, u32[]{:S(2)}) collective-permute-start(bf16[48,1024]{1,0:T(8,128)(2,1)S(1)} %get-tuple-element.52), channel_id=1, source_target_pairs={{0,4},{2,6},{4,8},{6,10},{8,12},{10,14},{12,0},{14,2},{1,5},{3,7},... | collective-permute-start | bytes 294920 | tf_op jit(solution)/shard_map/ppermute | solution.py:425
  21.4 7.1 %prepare.1 = (bf16[224,6144]{1,0:T(8,128)(2,1)S(1)}, bf16[224,6144]{1,0:T(8,128)(2,1)S(1)}, bf16[224,7168]{1,0:T(8,128)(2,1)S(1)}, bf16[224,1024]{1,0:T(8,128)(2,1)S(1)}) custom-call(s32[17]{0:T(128)S(1)} %dynamic-slice_bitcast_fusion.ids_ref, bf16[224,6144]{1,0:T(8,128)(2,1)} %bitcast.22, bf16[224,6144]{1,0:T(8,128)(2,1)} %bitcast.23, ...), custom_call_target="tpu_custom_call" | custom-call | flops 4000000000 | bytes 13762560 | tf_op jit(solution)/shard_map/prepare/pallas_call | solution.py:130
  28.6 0.0 collective-permute-done.4.refs_4_
  28.6 2.2 %collective-permute-done.6.refs_6_ = bf16[48,1024]{1,0:T(8,128)(2,1)S(1)} collective-permute-done((bf16[48,1024]{1,0:T(8,128)(2,1)S(1)}, bf16[48,1024]{1,0:T(8,128)(2,1)S(1)}, u32[]{:S(2)}, u32[]{:S(2)}) %collective-permute-start.6) | collective-permute-done | bytes 98336 | tf_op jit(solution)/shard_map/ppermute | solution.py:425
  30.9 0.6 copy-done.9
  31.5 0.0 copy-done.10
  31.5 1.3 in_order.1.refs_0_.refs_4_
  32.8 1.8 %collective-permute-start.9 = (bf16[224,7168]{1,0:T(8,128)(2,1)S(1)}, bf16[224,7168]{1,0:T(8,128)(2,1)S(1)}, u32[]{:S(2)}, u32[]{:S(2)}) collective-permute-start(bf16[224,7168]{1,0:T(8,128)(2,1)S(1)} %get-tuple-element.71.refs_3_.own_ref), channel_id=1, source_target_pairs={{0,1},{1,0},{2,3},{3,2},{4,5},{5,4},{6,7},{7,6},{8,9},{9,8},{10,11... | collective-permute-start | bytes 9633800 | tf_op jit(solution)/shard_map/ppermute | solution.py:205
  34.6 1.3 collective-permute-start.7
  35.9 1.4 collective-permute-start.10
  37.3 2.5 %collective-permute-start.12 = (bf16[384,1024]{1,0:T(8,128)(2,1)S(1)}, bf16[384,1024]{1,0:T(8,128)(2,1)S(1)}, u32[]{:S(2)}, u32[]{:S(2)}) collective-permute-start(bf16[384,1024]{1,0:T(8,128)(2,1)S(1)} %in_order.1.refs_0_.refs_4_), channel_id=1, source_target_pairs={{0,192},{1,49},{16,208},{17,1},{32,224},{33,17},{48,240},{49,33},{... | collective-permute-start | bytes 2359304 | tf_op jit(solution)/shard_map/ppermute | solution.py:201
  39.8 8.8 %collective-permute-done.7.refs_1_.a_ref.refs_5_ = bf16[384,1024]{1,0:T(8,128)(2,1)S(1)} collective-permute-done((bf16[384,1024]{1,0:T(8,128)(2,1)S(1)}, bf16[384,1024]{1,0:T(8,128)(2,1)S(1)}, u32[]{:S(2)}, u32[]{:S(2)}) %collective-permute-start.7) | collective-permute-done | bytes 786464 | tf_op jit(solution)/shard_map/ppermute | solution.py:201
  48.6 1.6 %collective-permute-start.8 = (bf16[384,1024]{1,0:T(8,128)(2,1)S(1)}, bf16[384,1024]{1,0:T(8,128)(2,1)S(1)}, u32[]{:S(2)}, u32[]{:S(2)}) collective-permute-start(bf16[384,1024]{1,0:T(8,128)(2,1)S(1)} %collective-permute-done.7.refs_1_.a_ref.refs_5_), channel_id=1, source_target_pairs={{0,16},{1,65},{16,32},{17,81},{32,48},{33,97},{48,0},{49,113},{64,... | collective-permute-start | bytes 2359304 | tf_op jit(solution)/shard_map/ppermute | solution.py:201
  50.3 2.6 %collective-permute-done.10.refs_2_.b_ref.refs_6_ = bf16[384,1024]{1,0:T(8,128)(2,1)S(1)} collective-permute-done((bf16[384,1024]{1,0:T(8,128)(2,1)S(1)}, bf16[384,1024]{1,0:T(8,128)(2,1)S(1)}, u32[]{:S(2)}, u32[]{:S(2)}) %collective-permute-start.10) | collective-permute-done | bytes 786464 | tf_op jit(solution)/shard_map/ppermute | solution.py:201
  52.9 0.1 join.1
  53.0 2.5 %collective-permute-start.15 = (bf16[768,1024]{1,0:T(8,128)(2,1)S(1)}, bf16[768,1024]{1,0:T(8,128)(2,1)S(1)}, u32[]{:S(2)}, u32[]{:S(2)}) collective-permute-start(bf16[768,1024]{1,0:T(8,128)(2,1)S(1)} %join.1), channel_id=1, source_target_pairs={{0,64},{1,17},{16,80},{17,33},{32,96},{33,49},{48,112},{49,1},{64,... | collective-permute-start | bytes 4718600 | tf_op jit(solution)/shard_map/ppermute | solution.py:201
  55.6 0.7 collective-permute-done.12.refs_4_.refs_8_
  56.2 2.4 %collective-permute-start.20 = (bf16[768,1024]{1,0:T(8,128)(2,1)S(1)}, bf16[768,1024]{1,0:T(8,128)(2,1)S(1)}, u32[]{:S(2)}, u32[]{:S(2)}) collective-permute-start(bf16[768,1024]{1,0:T(8,128)(2,1)S(1)} %join.1), channel_id=1, source_target_pairs={{0,192},{1,49},{16,208},{17,1},{32,224},{33,17},{48,240},{49,33},{... | collective-permute-start | bytes 4718600 | tf_op jit(solution)/shard_map/ppermute | solution.py:201
  58.6 1.4 for_other.4
  60.1 1.0 collective-permute-start.16
  61.1 6.1 %collective-permute-done.8.refs_0_.refs_4_ = bf16[384,1024]{1,0:T(8,128)(2,1)S(1)} collective-permute-done((bf16[384,1024]{1,0:T(8,128)(2,1)S(1)}, bf16[384,1024]{1,0:T(8,128)(2,1)S(1)}, u32[]{:S(2)}, u32[]{:S(2)}) %collective-permute-start.8) | collective-permute-done | bytes 786464 | tf_op jit(solution)/shard_map/ppermute | solution.py:201
  67.1 1.2 collective-permute-start.13
  68.4 1.4 collective-permute-start.19
  69.8 1.0 collective-permute-start.14
  70.8 2.9 %down.3.refs_4_ = f32[448,1024]{1,0:T(8,128)S(1)} custom-call(s32[17]{0:T(128)S(1)} %dynamic-slice_bitcast_fusion.ids_ref, bf16[224,7168]{1,0:T(8,128)(2,1)S(1)} %get-tuple-element.71.refs_3_.own_ref, bf16[224,7168]{1,0:T(8,128)(2,1)S(1)} %collective-permute-done.9.give_ref.other_ref, bf16[384,1024]{1,0:T(8,128)(2,1)S(1)} %in_order.1.refs_0_.refs_4_, ...), custom_call_target="tpu_custom_call" | custom-call | flops 1000 | bytes 1000 | tf_op jit(solution)/shard_map/down/pallas_call | solution.py:276
  73.8 3.3 %act.3 = (bf16[224,6144]{1,0:T(8,128)(2,1)}, bf16[224,6144]{1,0:T(8,128)(2,1)}, f32[16,1,384]{2,1,0:T(1,128)S(1)}) custom-call(s32[17]{0:T(128)S(1)} %dynamic-slice_bitcast_fusion.ids_ref, bf16[224,1024]{1,0:T(8,128)(2,1)S(1)} %get-tuple-element.43.refs_0_, bf16[224,6144]{1,0:T(8,128)(2,1)S(1)} %get-tuple-element.44.refs_1_, ...), custom_call_target="tpu_custom_call" | custom-call | flops 1000 | bytes 1000 | tf_op jit(solution)/shard_map/act/pallas_call | solution.py:343
  77.1 4.4 %collective-permute-done.15.refs_2_.refs_6_ = bf16[768,1024]{1,0:T(8,128)(2,1)S(1)} collective-permute-done((bf16[768,1024]{1,0:T(8,128)(2,1)S(1)}, bf16[768,1024]{1,0:T(8,128)(2,1)S(1)}, u32[]{:S(2)}, u32[]{:S(2)}) %collective-permute-start.15) | collective-permute-done | bytes 1572896 | tf_op jit(solution)/shard_map/ppermute | solution.py:201
  81.5 8.1 %collective-permute-done.13.refs_0_.refs_4_ = bf16[384,1024]{1,0:T(8,128)(2,1)S(1)} collective-permute-done((bf16[384,1024]{1,0:T(8,128)(2,1)S(1)}, bf16[384,1024]{1,0:T(8,128)(2,1)S(1)}, u32[]{:S(2)}, u32[]{:S(2)}) %collective-permute-start.13) | collective-permute-done | bytes 786464 | tf_op jit(solution)/shard_map/ppermute | solution.py:201
  89.6 0.1 collective-permute-start.17
  89.7 1.7 %for_other.5 = bf16[6,224,384]{2,1,0:T(8,128)(2,1)S(1)} custom-call(bf16[224,7168]{1,0:T(8,128)(2,1)S(1)} %collective-permute-done.9.give_ref.other_ref, bf16[384,1024]{1,0:T(8,128)(2,1)S(1)} %collective-permute-done.8.refs_0_.refs_4_, bf16[384,1024]{1,0:T(8,128)(2,1)S(1)} %collective-permute-done.19.refs_1_.refs_5_, ...), custom_call_target="tpu_custom_call" | custom-call | flops 1000 | bytes 1000 | tf_op jit(solution)/shard_map/for_other/pallas_call | solution.py:230
  91.4 0.2 collective-permute-start.21
  91.7 1.2 collective-permute-done.14.refs_1_.refs_5_
  92.8 3.1 %collective-permute-start.18 = (bf16[384,1024]{1,0:T(8,128)(2,1)S(1)}, bf16[384,1024]{1,0:T(8,128)(2,1)S(1)}, u32[]{:S(2)}, u32[]{:S(2)}) collective-permute-start(bf16[384,1024]{1,0:T(8,128)(2,1)S(1)} %collective-permute-done.14.refs_1_.refs_5_), channel_id=1, source_target_pairs={{0,192},{1,49},{16,208},{17,1},{32,224},{33,17},{48,240},{49,33},{... | collective-permute-start | bytes 2359304 | tf_op jit(solution)/shard_map/ppermute | solution.py:201
  95.9 3.2 %down.4.refs_4_ = f32[448,1024]{1,0:T(8,128)S(1)} custom-call(s32[17]{0:T(128)S(1)} %dynamic-slice_bitcast_fusion.ids_ref, bf16[224,7168]{1,0:T(8,128)(2,1)S(1)} %get-tuple-element.71.refs_3_.own_ref, bf16[224,7168]{1,0:T(8,128)(2,1)S(1)} %collective-permute-done.9.give_ref.other_ref, bf16[384,1024]{1,0:T(8,128)(2,1)S(1)} %collective-permute-done.8.refs_0_.refs_4_, ...), custom_call_target="tpu_custom_call" | custom-call | flops 1000 | bytes 1000 | tf_op jit(solution)/shard_map/down/pallas_call | solution.py:276
  99.2 3.7 %act.4 = (bf16[224,6144]{1,0:T(8,128)(2,1)}, bf16[224,6144]{1,0:T(8,128)(2,1)}, f32[16,1,384]{2,1,0:T(1,128)S(1)}) custom-call(s32[17]{0:T(128)S(1)} %dynamic-slice_bitcast_fusion.ids_ref, bf16[224,1024]{1,0:T(8,128)(2,1)S(1)} %get-tuple-element.43.refs_0_, ...), custom_call_target="tpu_custom_call", output_to_operand_aliasing={{0}: (10, {}), {1}: (11, {})} | custom-call | flops 1000 | bytes 1000 | tf_op jit(solution)/shard_map/act/pallas_call | solution.py:343
  102.9 2.0 %collective-permute-done.18.refs_2_.refs_7_.refs_3_ = bf16[384,1024]{1,0:T(8,128)(2,1)S(1)} collective-permute-done((bf16[384,1024]{1,0:T(8,128)(2,1)S(1)}, bf16[384,1024]{1,0:T(8,128)(2,1)S(1)}, u32[]{:S(2)}, u32[]{:S(2)}) %collective-permute-start.18) | collective-permute-done | bytes 786464 | tf_op jit(solution)/shard_map/ppermute | solution.py:201
  104.9 0.9 for_other.6
  105.8 4.1 %collective-permute-start.22 = (bf16[3,224,384]{2,1,0:T(8,128)(2,1)S(1)}, bf16[3,224,384]{2,1,0:T(8,128)(2,1)S(1)}, u32[]{:S(2)}, u32[]{:S(2)}) collective-permute-start(bf16[3,224,384]{2,1,0:T(8,128)(2,1)S(1)} %for_other.6), channel_id=1, source_target_pairs={{0,1},{1,0},{2,3},{3,2},{4,5},{5,4},{6,7},{7,6},{8,9},{9,8},{10,11... | collective-permute-start | bytes 1548296 | tf_op jit(solution)/shard_map/ppermute | solution.py:205
  109.9 1.5 %collective-permute-done.22.refs_8_ = bf16[3,224,384]{2,1,0:T(8,128)(2,1)S(1)} collective-permute-done((bf16[3,224,384]{2,1,0:T(8,128)(2,1)S(1)}, bf16[3,224,384]{2,1,0:T(8,128)(2,1)S(1)}, u32[]{:S(2)}, u32[]{:S(2)}) %collective-permute-start.22) | collective-permute-done | bytes 516128 | tf_op jit(solution)/shard_map/ppermute | solution.py:205
  111.4 0.7 for_other.7
  112.1 0.5 collective-permute-start.23
  112.6 2.9 %down.5 = (bf16[224,1024]{1,0:T(8,128)(2,1)S(1)}, bf16[224,1024]{1,0:T(8,128)(2,1)S(1)}) custom-call(s32[17]{0:T(128)S(1)} %dynamic-slice_bitcast_fusion.ids_ref, bf16[224,7168]{1,0:T(8,128)(2,1)S(1)} %get-tuple-element.71.refs_3_.own_ref, bf16[224,7168]{1,0:T(8,128)(2,1)S(1)} %collective-permute-done.9.give_ref.other_ref, ...), custom_call_target="tpu_custom_call" | custom-call | flops 2000000000 | bytes 1000 | tf_op jit(solution)/shard_map/down/pallas_call | solution.py:276
  115.5 0.0 copy-start.1
  115.5 0.0 copy-start.2
  115.6 3.4 %act.5 = (bf16[224,6144]{1,0:T(8,128)(2,1)}, bf16[224,6144]{1,0:T(8,128)(2,1)}, f32[16,1,384]{2,1,0:T(1,128)S(1)}) custom-call(s32[17]{0:T(128)S(1)} %dynamic-slice_bitcast_fusion.ids_ref, bf16[224,1024]{1,0:T(8,128)(2,1)S(1)} %get-tuple-element.43.refs_0_, ...), custom_call_target="tpu_custom_call", output_to_operand_aliasing={{0}: (11, {}), {1}: (12, {})} | custom-call | flops 1000 | bytes 1000 | tf_op jit(solution)/shard_map/act/pallas_call | solution.py:343
  118.9 0.3 collective-permute-start.24
  119.2 13.1 %all_to_all.17 = f32[16,1,384]{2,1,0:T(1,128)S(1)} all-to-all(f32[16,1,384]{2,1,0:T(1,128)S(1)} %get-tuple-element.74), channel_id=1, replica_groups=mesh['dp'=16,'expert'=8,'tensor'=2] {'dp'}, dimensions={0} | all-to-all | bytes 49152 | tf_op jit(solution)/shard_map/all_to_all | solution.py:487
  132.3 3.3 %all-gather.1 = f32[2,1,384]{2,1,0:T(1,128)S(1)} all-gather(f32[1,1,384]{2,1,0:T(1,128)S(1)} %reshape.21), channel_id=2, replica_groups=mesh['dp'=16,'expert'=8,'tensor'=2] {'tensor'}, dimensions={0}, use_global_device_ids=true | all-gather | bytes 4608 | tf_op jit(solution)/shard_map/all_gather | solution.py:488
  135.6 0.1 all_to_all.12
  135.7 11.0 %all_to_all.18 = f32[8,1,48]{2,1,0:T(1,128)S(1)} all-to-all(f32[8,1,48]{2,1,0:T(1,128)S(1)} %all_to_all.12), channel_id=1, replica_groups=mesh['dp'=16,'expert'=8,'tensor'=2] {'expert'}, dimensions={0} | all-to-all | bytes 3072 | tf_op jit(solution)/shard_map/all_to_all | solution.py:489
  146.7 0.7 unpack.1
  147.4 1.5 %finish.1 = bf16[224,2048]{1,0:T(8,128)(2,1)} custom-call(s32[17]{0:T(128)S(1)} %dynamic-slice_bitcast_fusion.ids_ref, bf16[224,1024]{1,0:T(8,128)(2,1)S(1)} %get-tuple-element.72.mine_ref, bf16[224,1024]{1,0:T(8,128)(2,1)S(1)} %collective-permute-done.24.theirs_ref), custom_call_target="tpu_custom_call" | custom-call | flops 1000 | bytes 1000 | tf_op jit(solution)/shard_map/finish/pallas_call | solution.py:297
  (32 shorter events, 0.1 us)
Async XLA Ops:
  1.3 0.7 copy-start.3
  3.5 0.6 copy-start
  4.2 14.9 %collective-permute-start = (bf16[48,1024]{1,0:T(8,128)(2,1)S(1)}, bf16[48,1024]{1,0:T(8,128)(2,1)S(1)}, u32[]{:S(2)}, u32[]{:S(2)}) collective-permute-start(bf16[48,1024]{1,0:T(8,128)(2,1)S(1)} %get-tuple-element.49), channel_id=1, source_target_pairs={{0,2},{2,4},{4,6},{6,8},{8,10},{10,12},{12,14},{14,0},{1,3},{3,5},... | collective-permute-start | bytes 294920 | tf_op jit(solution)/shard_map/ppermute | solution.py:425
  6.6 12.4 %collective-permute-start.1 = (bf16[48,1024]{1,0:T(8,128)(2,1)S(1)}, bf16[48,1024]{1,0:T(8,128)(2,1)S(1)}, u32[]{:S(2)}, u32[]{:S(2)}) collective-permute-start(bf16[48,1024]{1,0:T(8,128)(2,1)S(1)} %get-tuple-element.51), channel_id=1, source_target_pairs={{0,14},{2,0},{4,2},{6,4},{8,6},{10,8},{12,10},{14,12},{1,15},{3,1}... | collective-permute-start | bytes 294920 | tf_op jit(solution)/shard_map/ppermute | solution.py:425
  10.6 18.0 %collective-permute-start.3 = (bf16[48,1024]{1,0:T(8,128)(2,1)S(1)}, bf16[48,1024]{1,0:T(8,128)(2,1)S(1)}, u32[]{:S(2)}, u32[]{:S(2)}) collective-permute-start(bf16[48,1024]{1,0:T(8,128)(2,1)S(1)} %get-tuple-element.53), channel_id=1, source_target_pairs={{0,6},{2,8},{4,10},{6,12},{8,14},{10,0},{12,2},{14,4},{1,7},{3,9},... | collective-permute-start | bytes 294920 | tf_op jit(solution)/shard_map/ppermute | solution.py:425
  12.2 16.4 %collective-permute-start.4 = (bf16[48,1024]{1,0:T(8,128)(2,1)S(1)}, bf16[48,1024]{1,0:T(8,128)(2,1)S(1)}, u32[]{:S(2)}, u32[]{:S(2)}) collective-permute-start(bf16[48,1024]{1,0:T(8,128)(2,1)S(1)} %get-tuple-element.54), channel_id=1, source_target_pairs={{0,8},{2,10},{4,12},{6,14},{8,0},{10,2},{12,4},{14,6},{1,9},{3,11}... | collective-permute-start | bytes 294920 | tf_op jit(solution)/shard_map/ppermute | solution.py:425
  15.0 13.6 %collective-permute-start.5 = (bf16[48,1024]{1,0:T(8,128)(2,1)S(1)}, bf16[48,1024]{1,0:T(8,128)(2,1)S(1)}, u32[]{:S(2)}, u32[]{:S(2)}) collective-permute-start(bf16[48,1024]{1,0:T(8,128)(2,1)S(1)} %get-tuple-element.55), channel_id=1, source_target_pairs={{0,10},{2,12},{4,14},{6,0},{8,2},{10,4},{12,6},{14,8},{1,11},{3,13... | collective-permute-start | bytes 294920 | tf_op jit(solution)/shard_map/ppermute | solution.py:425
  19.1 9.5 %copy-start.4 = (bf16[48,1024]{1,0:T(8,128)(2,1)}, bf16[48,1024]{1,0:T(8,128)(2,1)S(1)}, u32[]{:S(2)}) copy-start(bf16[48,1024]{1,0:T(8,128)(2,1)S(1)} %collective-permute-done.refs_1_) | copy-start | bytes 294916
  19.1 11.8 %collective-permute-start.6 = (bf16[48,1024]{1,0:T(8,128)(2,1)S(1)}, bf16[48,1024]{1,0:T(8,128)(2,1)S(1)}, u32[]{:S(2)}, u32[]{:S(2)}) collective-permute-start(bf16[48,1024]{1,0:T(8,128)(2,1)S(1)} %get-tuple-element.57), channel_id=1, source_target_pairs={{0,12},{2,14},{4,0},{6,2},{8,4},{10,6},{12,8},{14,10},{1,13},{3,15... | collective-permute-start | bytes 294920 | tf_op jit(solution)/shard_map/ppermute | solution.py:425
  19.1 9.5 %copy-start.5 = (bf16[48,1024]{1,0:T(8,128)(2,1)}, bf16[48,1024]{1,0:T(8,128)(2,1)S(1)}, u32[]{:S(2)}) copy-start(bf16[48,1024]{1,0:T(8,128)(2,1)S(1)} %collective-permute-done.1.refs_7_) | copy-start | bytes 294916
  19.1 11.8 %collective-permute-start.2 = (bf16[48,1024]{1,0:T(8,128)(2,1)S(1)}, bf16[48,1024]{1,0:T(8,128)(2,1)S(1)}, u32[]{:S(2)}, u32[]{:S(2)}) collective-permute-start(bf16[48,1024]{1,0:T(8,128)(2,1)S(1)} %get-tuple-element.52), channel_id=1, source_target_pairs={{0,4},{2,6},{4,8},{6,10},{8,12},{10,14},{12,0},{14,2},{1,5},{3,7},... | collective-permute-start | bytes 294920 | tf_op jit(solution)/shard_map/ppermute | solution.py:425
  28.6 2.3 %copy-start.6 = (bf16[48,1024]{1,0:T(8,128)(2,1)}, bf16[48,1024]{1,0:T(8,128)(2,1)S(1)}, u32[]{:S(2)}) copy-start(bf16[48,1024]{1,0:T(8,128)(2,1)S(1)} %collective-permute-done.3.refs_3_) | copy-start | bytes 294916
  28.6 2.3 %copy-start.7 = (bf16[48,1024]{1,0:T(8,128)(2,1)}, bf16[48,1024]{1,0:T(8,128)(2,1)S(1)}, u32[]{:S(2)}) copy-start(bf16[48,1024]{1,0:T(8,128)(2,1)S(1)} %collective-permute-done.4.refs_4_) | copy-start | bytes 294916
  28.6 2.3 %copy-start.8 = (bf16[48,1024]{1,0:T(8,128)(2,1)}, bf16[48,1024]{1,0:T(8,128)(2,1)S(1)}, u32[]{:S(2)}) copy-start(bf16[48,1024]{1,0:T(8,128)(2,1)S(1)} %collective-permute-done.5.refs_5_) | copy-start | bytes 294916
  30.9 0.6 copy-start.9
  30.9 0.7 copy-start.10
  32.8 25.8 %collective-permute-start.9 = (bf16[224,7168]{1,0:T(8,128)(2,1)S(1)}, bf16[224,7168]{1,0:T(8,128)(2,1)S(1)}, u32[]{:S(2)}, u32[]{:S(2)}) collective-permute-start(bf16[224,7168]{1,0:T(8,128)(2,1)S(1)} %get-tuple-element.71.refs_3_.own_ref), channel_id=1, source_target_pairs={{0,1},{1,0},{2,3},{3,2},{4,5},{5,4},{6,7},{7,6},{8,9},{9,8},{10,11... | collective-permute-start | bytes 9633800 | tf_op jit(solution)/shard_map/ppermute | solution.py:205
  34.6 14.0 %collective-permute-start.7 = (bf16[384,1024]{1,0:T(8,128)(2,1)S(1)}, bf16[384,1024]{1,0:T(8,128)(2,1)S(1)}, u32[]{:S(2)}, u32[]{:S(2)}) collective-permute-start(bf16[384,1024]{1,0:T(8,128)(2,1)S(1)} %in_order.1.refs_0_.refs_4_), channel_id=1, source_target_pairs={{0,16},{1,65},{16,32},{17,81},{32,48},{33,97},{48,0},{49,113},{64,... | collective-permute-start | bytes 2359304 | tf_op jit(solution)/shard_map/ppermute | solution.py:201
  35.9 17.0 %collective-permute-start.10 = (bf16[384,1024]{1,0:T(8,128)(2,1)S(1)}, bf16[384,1024]{1,0:T(8,128)(2,1)S(1)}, u32[]{:S(2)}, u32[]{:S(2)}) collective-permute-start(bf16[384,1024]{1,0:T(8,128)(2,1)S(1)} %in_order.1.refs_0_.refs_4_), channel_id=1, source_target_pairs={{0,48},{1,193},{16,0},{17,209},{32,16},{33,225},{48,32},{49,241},{... | collective-permute-start | bytes 2359304 | tf_op jit(solution)/shard_map/ppermute | solution.py:201
  37.3 18.9 %collective-permute-start.12 = (bf16[384,1024]{1,0:T(8,128)(2,1)S(1)}, bf16[384,1024]{1,0:T(8,128)(2,1)S(1)}, u32[]{:S(2)}, u32[]{:S(2)}) collective-permute-start(bf16[384,1024]{1,0:T(8,128)(2,1)S(1)} %in_order.1.refs_0_.refs_4_), channel_id=1, source_target_pairs={{0,192},{1,49},{16,208},{17,1},{32,224},{33,17},{48,240},{49,33},{... | collective-permute-start | bytes 2359304 | tf_op jit(solution)/shard_map/ppermute | solution.py:201
  39.8 18.8 %collective-permute-start.11 = (bf16[384,1024]{1,0:T(8,128)(2,1)S(1)}, bf16[384,1024]{1,0:T(8,128)(2,1)S(1)}, u32[]{:S(2)}, u32[]{:S(2)}) collective-permute-start(bf16[384,1024]{1,0:T(8,128)(2,1)S(1)} %in_order.1.refs_0_.refs_4_), channel_id=1, source_target_pairs={{0,64},{1,17},{16,80},{17,33},{32,96},{33,49},{48,112},{49,1},{64,... | collective-permute-start | bytes 2359304 | tf_op jit(solution)/shard_map/ppermute | solution.py:201
  48.6 18.5 %collective-permute-start.8 = (bf16[384,1024]{1,0:T(8,128)(2,1)S(1)}, bf16[384,1024]{1,0:T(8,128)(2,1)S(1)}, u32[]{:S(2)}, u32[]{:S(2)}) collective-permute-start(bf16[384,1024]{1,0:T(8,128)(2,1)S(1)} %collective-permute-done.7.refs_1_.a_ref.refs_5_), channel_id=1, source_target_pairs={{0,16},{1,65},{16,32},{17,81},{32,48},{33,97},{48,0},{49,113},{64,... | collective-permute-start | bytes 2359304 | tf_op jit(solution)/shard_map/ppermute | solution.py:201
  53.0 28.5 %collective-permute-start.15 = (bf16[768,1024]{1,0:T(8,128)(2,1)S(1)}, bf16[768,1024]{1,0:T(8,128)(2,1)S(1)}, u32[]{:S(2)}, u32[]{:S(2)}) collective-permute-start(bf16[768,1024]{1,0:T(8,128)(2,1)S(1)} %join.1), channel_id=1, source_target_pairs={{0,64},{1,17},{16,80},{17,33},{32,96},{33,49},{48,112},{49,1},{64,... | collective-permute-start | bytes 4718600 | tf_op jit(solution)/shard_map/ppermute | solution.py:201
  56.2 33.5 %collective-permute-start.20 = (bf16[768,1024]{1,0:T(8,128)(2,1)S(1)}, bf16[768,1024]{1,0:T(8,128)(2,1)S(1)}, u32[]{:S(2)}, u32[]{:S(2)}) collective-permute-start(bf16[768,1024]{1,0:T(8,128)(2,1)S(1)} %join.1), channel_id=1, source_target_pairs={{0,192},{1,49},{16,208},{17,1},{32,224},{33,17},{48,240},{49,33},{... | collective-permute-start | bytes 4718600 | tf_op jit(solution)/shard_map/ppermute | solution.py:201
  60.1 9.8 %collective-permute-start.16 = (bf16[5,224,384]{2,1,0:T(8,128)(2,1)S(1)}, bf16[5,224,384]{2,1,0:T(8,128)(2,1)S(1)}, u32[]{:S(2)}, u32[]{:S(2)}) collective-permute-start(bf16[5,224,384]{2,1,0:T(8,128)(2,1)S(1)} %for_other.4), channel_id=1, source_target_pairs={{0,1},{1,0},{2,3},{3,2},{4,5},{5,4},{6,7},{7,6},{8,9},{9,8},{10,11... | collective-permute-start | bytes 2580488 | tf_op jit(solution)/shard_map/ppermute | solution.py:205
  67.1 22.5 %collective-permute-start.13 = (bf16[384,1024]{1,0:T(8,128)(2,1)S(1)}, bf16[384,1024]{1,0:T(8,128)(2,1)S(1)}, u32[]{:S(2)}, u32[]{:S(2)}) collective-permute-start(bf16[384,1024]{1,0:T(8,128)(2,1)S(1)} %collective-permute-done.8.refs_0_.refs_4_), channel_id=1, source_target_pairs={{0,64},{1,17},{16,80},{17,33},{32,96},{33,49},{48,112},{49,1},{64,... | collective-permute-start | bytes 2359304 | tf_op jit(solution)/shard_map/ppermute | solution.py:201
  68.4 21.3 %collective-permute-start.19 = (bf16[384,1024]{1,0:T(8,128)(2,1)S(1)}, bf16[384,1024]{1,0:T(8,128)(2,1)S(1)}, u32[]{:S(2)}, u32[]{:S(2)}) collective-permute-start(bf16[384,1024]{1,0:T(8,128)(2,1)S(1)} %collective-permute-done.12.refs_4_.refs_8_), channel_id=1, source_target_pairs={{0,192},{1,49},{16,208},{17,1},{32,224},{33,17},{48,240},{49,33},{... | collective-permute-start | bytes 2359304 | tf_op jit(solution)/shard_map/ppermute | solution.py:201
  69.8 23.0 %collective-permute-start.14 = (bf16[384,1024]{1,0:T(8,128)(2,1)S(1)}, bf16[384,1024]{1,0:T(8,128)(2,1)S(1)}, u32[]{:S(2)}, u32[]{:S(2)}) collective-permute-start(bf16[384,1024]{1,0:T(8,128)(2,1)S(1)} %collective-permute-done.8.refs_0_.refs_4_), channel_id=1, source_target_pairs={{0,192},{1,49},{16,208},{17,1},{32,224},{33,17},{48,240},{49,33},{... | collective-permute-start | bytes 2359304 | tf_op jit(solution)/shard_map/ppermute | solution.py:201
  89.6 21.8 %collective-permute-start.17 = (bf16[768,1024]{1,0:T(8,128)(2,1)S(1)}, bf16[768,1024]{1,0:T(8,128)(2,1)S(1)}, u32[]{:S(2)}, u32[]{:S(2)}) collective-permute-start(bf16[768,1024]{1,0:T(8,128)(2,1)S(1)} %collective-permute-done.15.refs_2_.refs_6_), channel_id=1, source_target_pairs={{0,64},{1,17},{16,80},{17,33},{32,96},{33,49},{48,112},{49,1},{64,... | collective-permute-start | bytes 4718600 | tf_op jit(solution)/shard_map/ppermute | solution.py:201
  91.4 7.7 %collective-permute-start.21 = (bf16[6,224,384]{2,1,0:T(8,128)(2,1)S(1)}, bf16[6,224,384]{2,1,0:T(8,128)(2,1)S(1)}, u32[]{:S(2)}, u32[]{:S(2)}) collective-permute-start(bf16[6,224,384]{2,1,0:T(8,128)(2,1)S(1)} %for_other.5), channel_id=1, source_target_pairs={{0,1},{1,0},{2,3},{3,2},{4,5},{5,4},{6,7},{7,6},{8,9},{9,8},{10,11... | collective-permute-start | bytes 3096584 | tf_op jit(solution)/shard_map/ppermute | solution.py:205
  92.8 12.1 %collective-permute-start.18 = (bf16[384,1024]{1,0:T(8,128)(2,1)S(1)}, bf16[384,1024]{1,0:T(8,128)(2,1)S(1)}, u32[]{:S(2)}, u32[]{:S(2)}) collective-permute-start(bf16[384,1024]{1,0:T(8,128)(2,1)S(1)} %collective-permute-done.14.refs_1_.refs_5_), channel_id=1, source_target_pairs={{0,192},{1,49},{16,208},{17,1},{32,224},{33,17},{48,240},{49,33},{... | collective-permute-start | bytes 2359304 | tf_op jit(solution)/shard_map/ppermute | solution.py:201
  105.8 5.6 %collective-permute-start.22 = (bf16[3,224,384]{2,1,0:T(8,128)(2,1)S(1)}, bf16[3,224,384]{2,1,0:T(8,128)(2,1)S(1)}, u32[]{:S(2)}, u32[]{:S(2)}) collective-permute-start(bf16[3,224,384]{2,1,0:T(8,128)(2,1)S(1)} %for_other.6), channel_id=1, source_target_pairs={{0,1},{1,0},{2,3},{3,2},{4,5},{5,4},{6,7},{7,6},{8,9},{9,8},{10,11... | collective-permute-start | bytes 1548296 | tf_op jit(solution)/shard_map/ppermute | solution.py:205
  112.1 3.4 %collective-permute-start.23 = (bf16[2,224,384]{2,1,0:T(8,128)(2,1)S(1)}, bf16[2,224,384]{2,1,0:T(8,128)(2,1)S(1)}, u32[]{:S(2)}, u32[]{:S(2)}) collective-permute-start(bf16[2,224,384]{2,1,0:T(8,128)(2,1)S(1)} %for_other.7), channel_id=1, source_target_pairs={{0,1},{1,0},{2,3},{3,2},{4,5},{5,4},{6,7},{7,6},{8,9},{9,8},{10,11... | collective-permute-start | bytes 1032200 | tf_op jit(solution)/shard_map/ppermute | solution.py:205
  115.5 31.1 %copy-start.1 = (s32[128,2]{0,1:T(2,128)S(1)}, s32[128,2]{0,1:T(2,128)}, u32[]{:S(2)}) copy-start(s32[128,2]{0,1:T(2,128)} %param.12) | copy-start | bytes 3076
  115.5 31.1 %copy-start.2 = (bf16[128,2]{0,1:T(2,128)(2,1)S(1)}, bf16[128,2]{0,1:T(2,128)(2,1)}, u32[]{:S(2)}) copy-start(bf16[128,2]{0,1:T(2,128)(2,1)} %param.13) | copy-start | bytes 1540
  118.9 28.5 %collective-permute-start.24 = (bf16[224,1024]{1,0:T(8,128)(2,1)S(1)}, bf16[224,1024]{1,0:T(8,128)(2,1)S(1)}, u32[]{:S(2)}, u32[]{:S(2)}) collective-permute-start(bf16[224,1024]{1,0:T(8,128)(2,1)S(1)} %get-tuple-element.75), channel_id=1, source_target_pairs={{0,1},{1,0},{2,3},{3,2},{4,5},{5,4},{6,7},{7,6},{8,9},{9,8},{10,11... | collective-permute-start | bytes 1376264 | tf_op jit(solution)/shard_map/ppermute | solution.py:205

commit v2 on v1

--- a/solution.py
+++ b/solution.py
@@ -379,7 +379,7 @@
 ACT = (
     ((0, 0), (1, 0), (-1, 0), (0, 1), (0, -1)),
     ((2, 0), (0, 2), (1, 1), (-1, 1), (1, -1), (-1, -1)),
-    ((2, 1), (2, -1), (1, 2), (-1, 2), (2, 2)),
+    ((2, 1), (2, -1), (2, 2), (1, 2), (-1, 2)),
 )
 OTHER = (ACT[0], ACT[1], ((2, 1), (2, -1), (2, 2)), ((1, 2), (-1, 2)))
 LABELS = sum(ACT, ())
@@ -451,11 +451,10 @@
             [parts[g] for g in need], where, held,
         )
 
-    def accumulate(step, acc, *others):
-        blocks = [b[l] for l in ACT[step]]
-        start = sum(len(a) for a in ACT[:step])
+    def accumulate(labels, acc, last, *others):
+        blocks = [b[l] for l in labels]
         own = after(give, *others) if others else give
-        return down(ids, start, own, got, rows, blocks, acc, step == len(ACT) - 1)
+        return down(ids, LABELS.index(labels[0]), own, got, rows, blocks, acc, last)
 
     right, left = hop(block, 1, 0), hop(block, -1, 0)
     up_one, down_one = hop(block, 0, 1), hop(block, 0, -1)
@@ -471,16 +470,16 @@
     far_up, far_down = hop(after(far, raw), 0, 1), hop(after(far, raw), 0, -1)
     b[2, 1], b[2, -1] = (far_up, 0), (far_down, 0)
     held = activate(0, held)
-    acc = accumulate(0, None)
+    acc = accumulate(ACT[0], None, False)
     pair_far = hop(after(pair_up, held[2], acc, far_up), 0, 1)
     b[1, 2], b[-1, 2] = (pair_far, 0), (pair_far, rows)
     b[2, 2] = (hop(far_down, 0, -1), 0)
     share(1)
     held = activate(1, held)
-    acc = accumulate(1, acc)
+    acc = accumulate(ACT[1] + ACT[2][:2], acc, False)
     share(2, held[2], acc)
     raw = share(3, parts[2])
-    mine, theirs = accumulate(2, acc, raw)
+    mine, theirs = accumulate(ACT[2][2:], acc, True, raw)
     gate_out, up_out, probe = activate(2, held)
     grad_down = finish(ids, mine, swap(after(theirs, probe)))
 

time: 149 us -> 149 us (level)
  no operation moved by 1% of the time
where the time goes in v2:
time: 149 us; the launch traced here: 148 us
  starting transfers between devices  43.6 us (29%)
  waiting for transfers between devices  36.9 us (25%)
  Pallas kernels  36.6 us (25%)
  blocking collectives  27.4 us (18%)
  local copies, waits for them, and re-layouts  2.76 us (2%)
    ppermute x12, waiting for transfers between devices, hop(): return lax.ppermute(array, ('dp', 'tensor'), shifts(first, second))  33.1 us
    ppermute x12, starting transfers between devices, hop(): return lax.ppermute(array, ('dp', 'tensor'), shifts(first, second))  18.6 us
    ppermute x7, starting transfers between devices, local(): lax.ppermute(chunk, 'expert', [(i, (i + k) % experts) for i in range(expe...  17.2 us
    all_to_all x1, blocking collectives, local(): lax.all_to_all(probe.reshape(columns, rows), 'dp', 0, 0, tiled=True)  13.1 us
    all_to_all x1, blocking collectives, local(): lax.all_to_all(totals.reshape(experts, cap), 'expert', 0, 0, tiled=True)  11 us
    pallas_call x3, Pallas kernels, act(): pl.pallas_call(functools.partial(act_kernel, at, n, rows, start, where, g...  10.4 us
    pallas_call x3, Pallas kernels, down(): pl.pallas_call(functools.partial(down_kernel, at, n, rows, start, first,...  9.13 us
    ppermute x6, starting transfers between devices, swap(): return lax.ppermute(array, 'tensor', [(0, 1), (1, 0)])  7.79 us
  transfers between devices with their start and end apart: 25, of which 10 were waited for; matrix products, arithmetic and copies ran while one was open for 0% of the time, Pallas kernels for 19%

profile of v2, /device:TPU:1, one launch (start us, length us, event | category | flops | bytes accessed | tf_op | source)
XLA Modules:
  0.0 148.2 jit_solution(17699832091846499468)
XLA Ops:
  0.6 0.7 dynamic-slice_bitcast_fusion.ids_ref
  1.3 0.7 copy-done.3
  2.0 1.5 %pack.1 = (bf16[48,1024]{1,0:T(8,128)(2,1)S(1)}, bf16[48,1024]{1,0:T(8,128)(2,1)S(1)}, bf16[48,1024]{1,0:T(8,128)(2,1)S(1)}, bf16[48,1024]{1,0:T(8,128)(2,1)S(1)...) custom-call(s32[1]{0:T(128)} %bitcast.3.z_ref.e_ref, ...), custom_call_target="tpu_custom_call" | custom-call | flops 1000 | bytes 1000 | tf_op jit(solution)/shard_map/pack/pallas_call | solution.py:68
  3.5 0.0 copy-start
  3.5 0.6 copy-done
  4.2 2.5 %collective-permute-start = (bf16[48,1024]{1,0:T(8,128)(2,1)S(1)}, bf16[48,1024]{1,0:T(8,128)(2,1)S(1)}, u32[]{:S(2)}, u32[]{:S(2)}) collective-permute-start(bf16[48,1024]{1,0:T(8,128)(2,1)S(1)} %get-tuple-element.49), channel_id=1, source_target_pairs={{0,2},{2,4},{4,6},{6,8},{8,10},{10,12},{12,14},{14,0},{1,3},{3,5},... | collective-permute-start | bytes 294920 | tf_op jit(solution)/shard_map/ppermute | solution.py:425
  6.6 3.9 %collective-permute-start.1 = (bf16[48,1024]{1,0:T(8,128)(2,1)S(1)}, bf16[48,1024]{1,0:T(8,128)(2,1)S(1)}, u32[]{:S(2)}, u32[]{:S(2)}) collective-permute-start(bf16[48,1024]{1,0:T(8,128)(2,1)S(1)} %get-tuple-element.51), channel_id=1, source_target_pairs={{0,14},{2,0},{4,2},{6,4},{8,6},{10,8},{12,10},{14,12},{1,15},{3,1}... | collective-permute-start | bytes 294920 | tf_op jit(solution)/shard_map/ppermute | solution.py:425
  10.6 1.6 %collective-permute-start.3 = (bf16[48,1024]{1,0:T(8,128)(2,1)S(1)}, bf16[48,1024]{1,0:T(8,128)(2,1)S(1)}, u32[]{:S(2)}, u32[]{:S(2)}) collective-permute-start(bf16[48,1024]{1,0:T(8,128)(2,1)S(1)} %get-tuple-element.53), channel_id=1, source_target_pairs={{0,6},{2,8},{4,10},{6,12},{8,14},{10,0},{12,2},{14,4},{1,7},{3,9},... | collective-permute-start | bytes 294920 | tf_op jit(solution)/shard_map/ppermute | solution.py:425
  12.2 2.8 %collective-permute-start.4 = (bf16[48,1024]{1,0:T(8,128)(2,1)S(1)}, bf16[48,1024]{1,0:T(8,128)(2,1)S(1)}, u32[]{:S(2)}, u32[]{:S(2)}) collective-permute-start(bf16[48,1024]{1,0:T(8,128)(2,1)S(1)} %get-tuple-element.54), channel_id=1, source_target_pairs={{0,8},{2,10},{4,12},{6,14},{8,0},{10,2},{12,4},{14,6},{1,9},{3,11}... | collective-permute-start | bytes 294920 | tf_op jit(solution)/shard_map/ppermute | solution.py:425
  15.0 4.0 %collective-permute-start.5 = (bf16[48,1024]{1,0:T(8,128)(2,1)S(1)}, bf16[48,1024]{1,0:T(8,128)(2,1)S(1)}, u32[]{:S(2)}, u32[]{:S(2)}) collective-permute-start(bf16[48,1024]{1,0:T(8,128)(2,1)S(1)} %get-tuple-element.55), channel_id=1, source_target_pairs={{0,10},{2,12},{4,14},{6,0},{8,2},{10,4},{12,6},{14,8},{1,11},{3,13... | collective-permute-start | bytes 294920 | tf_op jit(solution)/shard_map/ppermute | solution.py:425
  19.1 0.0 collective-permute-done.refs_1_
  19.1 0.0 collective-permute-start.6
  19.1 2.3 %collective-permute-start.2 = (bf16[48,1024]{1,0:T(8,128)(2,1)S(1)}, bf16[48,1024]{1,0:T(8,128)(2,1)S(1)}, u32[]{:S(2)}, u32[]{:S(2)}) collective-permute-start(bf16[48,1024]{1,0:T(8,128)(2,1)S(1)} %get-tuple-element.52), channel_id=1, source_target_pairs={{0,4},{2,6},{4,8},{6,10},{8,12},{10,14},{12,0},{14,2},{1,5},{3,7},... | collective-permute-start | bytes 294920 | tf_op jit(solution)/shard_map/ppermute | solution.py:425
  21.4 7.1 %prepare.1 = (bf16[224,6144]{1,0:T(8,128)(2,1)S(1)}, bf16[224,6144]{1,0:T(8,128)(2,1)S(1)}, bf16[224,7168]{1,0:T(8,128)(2,1)S(1)}, bf16[224,1024]{1,0:T(8,128)(2,1)S(1)}) custom-call(s32[17]{0:T(128)S(1)} %dynamic-slice_bitcast_fusion.ids_ref, bf16[224,6144]{1,0:T(8,128)(2,1)} %bitcast.22, bf16[224,6144]{1,0:T(8,128)(2,1)} %bitcast.23, ...), custom_call_target="tpu_custom_call" | custom-call | flops 4000000000 | bytes 13762560 | tf_op jit(solution)/shard_map/prepare/pallas_call | solution.py:130
  28.6 0.0 collective-permute-done.4.refs_4_
  28.6 2.2 %collective-permute-done.6.refs_6_ = bf16[48,1024]{1,0:T(8,128)(2,1)S(1)} collective-permute-done((bf16[48,1024]{1,0:T(8,128)(2,1)S(1)}, bf16[48,1024]{1,0:T(8,128)(2,1)S(1)}, u32[]{:S(2)}, u32[]{:S(2)}) %collective-permute-start.6) | collective-permute-done | bytes 98336 | tf_op jit(solution)/shard_map/ppermute | solution.py:425
  30.9 0.6 copy-done.9
  31.5 0.0 copy-done.10
  31.5 1.3 in_order.1.refs_0_.refs_4_
  32.8 1.8 %collective-permute-start.9 = (bf16[224,7168]{1,0:T(8,128)(2,1)S(1)}, bf16[224,7168]{1,0:T(8,128)(2,1)S(1)}, u32[]{:S(2)}, u32[]{:S(2)}) collective-permute-start(bf16[224,7168]{1,0:T(8,128)(2,1)S(1)} %get-tuple-element.71.refs_3_.own_ref), channel_id=1, source_target_pairs={{0,1},{1,0},{2,3},{3,2},{4,5},{5,4},{6,7},{7,6},{8,9},{9,8},{10,11... | collective-permute-start | bytes 9633800 | tf_op jit(solution)/shard_map/ppermute | solution.py:205
  34.6 1.3 collective-permute-start.7
  35.9 1.4 collective-permute-start.10
  37.3 2.5 %collective-permute-start.12 = (bf16[384,1024]{1,0:T(8,128)(2,1)S(1)}, bf16[384,1024]{1,0:T(8,128)(2,1)S(1)}, u32[]{:S(2)}, u32[]{:S(2)}) collective-permute-start(bf16[384,1024]{1,0:T(8,128)(2,1)S(1)} %in_order.1.refs_0_.refs_4_), channel_id=1, source_target_pairs={{0,192},{1,49},{16,208},{17,1},{32,224},{33,17},{48,240},{49,33},{... | collective-permute-start | bytes 2359304 | tf_op jit(solution)/shard_map/ppermute | solution.py:201
  39.8 8.8 %collective-permute-done.7.refs_1_.a_ref.refs_5_ = bf16[384,1024]{1,0:T(8,128)(2,1)S(1)} collective-permute-done((bf16[384,1024]{1,0:T(8,128)(2,1)S(1)}, bf16[384,1024]{1,0:T(8,128)(2,1)S(1)}, u32[]{:S(2)}, u32[]{:S(2)}) %collective-permute-start.7) | collective-permute-done | bytes 786464 | tf_op jit(solution)/shard_map/ppermute | solution.py:201
  48.6 1.6 %collective-permute-start.8 = (bf16[384,1024]{1,0:T(8,128)(2,1)S(1)}, bf16[384,1024]{1,0:T(8,128)(2,1)S(1)}, u32[]{:S(2)}, u32[]{:S(2)}) collective-permute-start(bf16[384,1024]{1,0:T(8,128)(2,1)S(1)} %collective-permute-done.7.refs_1_.a_ref.refs_5_), channel_id=1, source_target_pairs={{0,16},{1,65},{16,32},{17,81},{32,48},{33,97},{48,0},{49,113},{64,... | collective-permute-start | bytes 2359304 | tf_op jit(solution)/shard_map/ppermute | solution.py:201
  50.3 2.6 %collective-permute-done.10.refs_2_.b_ref.refs_6_ = bf16[384,1024]{1,0:T(8,128)(2,1)S(1)} collective-permute-done((bf16[384,1024]{1,0:T(8,128)(2,1)S(1)}, bf16[384,1024]{1,0:T(8,128)(2,1)S(1)}, u32[]{:S(2)}, u32[]{:S(2)}) %collective-permute-start.10) | collective-permute-done | bytes 786464 | tf_op jit(solution)/shard_map/ppermute | solution.py:201
  52.9 0.1 join.1
  53.0 2.5 %collective-permute-start.16 = (bf16[768,1024]{1,0:T(8,128)(2,1)S(1)}, bf16[768,1024]{1,0:T(8,128)(2,1)S(1)}, u32[]{:S(2)}, u32[]{:S(2)}) collective-permute-start(bf16[768,1024]{1,0:T(8,128)(2,1)S(1)} %join.1), channel_id=1, source_target_pairs={{0,64},{1,17},{16,80},{17,33},{32,96},{33,49},{48,112},{49,1},{64,... | collective-permute-start | bytes 4718600 | tf_op jit(solution)/shard_map/ppermute | solution.py:201
  55.6 0.7 collective-permute-done.12.refs_4_.refs_8_
  56.2 2.4 %collective-permute-start.20 = (bf16[768,1024]{1,0:T(8,128)(2,1)S(1)}, bf16[768,1024]{1,0:T(8,128)(2,1)S(1)}, u32[]{:S(2)}, u32[]{:S(2)}) collective-permute-start(bf16[768,1024]{1,0:T(8,128)(2,1)S(1)} %join.1), channel_id=1, source_target_pairs={{0,192},{1,49},{16,208},{17,1},{32,224},{33,17},{48,240},{49,33},{... | collective-permute-start | bytes 4718600 | tf_op jit(solution)/shard_map/ppermute | solution.py:201
  58.6 1.4 for_other.4
  60.1 1.0 collective-permute-start.17
  61.1 6.1 %collective-permute-done.8.refs_0_.refs_4_ = bf16[384,1024]{1,0:T(8,128)(2,1)S(1)} collective-permute-done((bf16[384,1024]{1,0:T(8,128)(2,1)S(1)}, bf16[384,1024]{1,0:T(8,128)(2,1)S(1)}, u32[]{:S(2)}, u32[]{:S(2)}) %collective-permute-start.8) | collective-permute-done | bytes 786464 | tf_op jit(solution)/shard_map/ppermute | solution.py:201
  67.1 1.2 collective-permute-start.13
  68.4 1.4 collective-permute-start.19
  69.8 1.0 collective-permute-start.14
  70.8 2.9 %down.3.refs_6_ = f32[448,1024]{1,0:T(8,128)S(1)} custom-call(s32[17]{0:T(128)S(1)} %dynamic-slice_bitcast_fusion.ids_ref, bf16[224,7168]{1,0:T(8,128)(2,1)S(1)} %get-tuple-element.71.refs_3_.own_ref, bf16[224,7168]{1,0:T(8,128)(2,1)S(1)} %collective-permute-done.9.give_ref.other_ref, bf16[384,1024]{1,0:T(8,128)(2,1)S(1)} %in_order.1.refs_0_.refs_4_, ...), custom_call_target="tpu_custom_call" | custom-call | flops 1000 | bytes 1000 | tf_op jit(solution)/shard_map/down/pallas_call | solution.py:276
  73.8 3.3 %act.3 = (bf16[224,6144]{1,0:T(8,128)(2,1)}, bf16[224,6144]{1,0:T(8,128)(2,1)}, f32[16,1,384]{2,1,0:T(1,128)S(1)}) custom-call(s32[17]{0:T(128)S(1)} %dynamic-slice_bitcast_fusion.ids_ref, bf16[224,1024]{1,0:T(8,128)(2,1)S(1)} %get-tuple-element.43.refs_0_, bf16[224,6144]{1,0:T(8,128)(2,1)S(1)} %get-tuple-element.44.refs_1_, ...), custom_call_target="tpu_custom_call" | custom-call | flops 1000 | bytes 1000 | tf_op jit(solution)/shard_map/act/pallas_call | solution.py:343
  77.1 4.4 %collective-permute-done.16.refs_2_.refs_6_ = bf16[768,1024]{1,0:T(8,128)(2,1)S(1)} collective-permute-done((bf16[768,1024]{1,0:T(8,128)(2,1)S(1)}, bf16[768,1024]{1,0:T(8,128)(2,1)S(1)}, u32[]{:S(2)}, u32[]{:S(2)}) %collective-permute-start.16) | collective-permute-done | bytes 1572896 | tf_op jit(solution)/shard_map/ppermute | solution.py:201
  81.5 8.1 %collective-permute-done.13.refs_4_.refs_0_ = bf16[384,1024]{1,0:T(8,128)(2,1)S(1)} collective-permute-done((bf16[384,1024]{1,0:T(8,128)(2,1)S(1)}, bf16[384,1024]{1,0:T(8,128)(2,1)S(1)}, u32[]{:S(2)}, u32[]{:S(2)}) %collective-permute-start.13) | collective-permute-done | bytes 786464 | tf_op jit(solution)/shard_map/ppermute | solution.py:201
  89.6 0.1 collective-permute-start.18
  89.7 1.7 %for_other.5 = bf16[6,224,384]{2,1,0:T(8,128)(2,1)S(1)} custom-call(bf16[224,7168]{1,0:T(8,128)(2,1)S(1)} %collective-permute-done.9.give_ref.other_ref, bf16[384,1024]{1,0:T(8,128)(2,1)S(1)} %collective-permute-done.8.refs_0_.refs_4_, bf16[384,1024]{1,0:T(8,128)(2,1)S(1)} %collective-permute-done.19.refs_1_.refs_5_, ...), custom_call_target="tpu_custom_call" | custom-call | flops 1000 | bytes 1000 | tf_op jit(solution)/shard_map/for_other/pallas_call | solution.py:230
  91.4 0.2 collective-permute-start.21
  91.7 1.2 collective-permute-done.14.refs_5_.refs_1_
  92.8 3.1 %collective-permute-start.15 = (bf16[384,1024]{1,0:T(8,128)(2,1)S(1)}, bf16[384,1024]{1,0:T(8,128)(2,1)S(1)}, u32[]{:S(2)}, u32[]{:S(2)}) collective-permute-start(bf16[384,1024]{1,0:T(8,128)(2,1)S(1)} %collective-permute-done.14.refs_5_.refs_1_), channel_id=1, source_target_pairs={{0,192},{1,49},{16,208},{17,1},{32,224},{33,17},{48,240},{49,33},{... | collective-permute-start | bytes 2359304 | tf_op jit(solution)/shard_map/ppermute | solution.py:201
  95.9 4.0 %down.4.refs_2_ = f32[448,1024]{1,0:T(8,128)S(1)} custom-call(s32[17]{0:T(128)S(1)} %dynamic-slice_bitcast_fusion.ids_ref, bf16[224,7168]{1,0:T(8,128)(2,1)S(1)} %get-tuple-element.71.refs_3_.own_ref, bf16[224,7168]{1,0:T(8,128)(2,1)S(1)} %collective-permute-done.9.give_ref.other_ref, bf16[384,1024]{1,0:T(8,128)(2,1)S(1)} %collective-permute-done.8.refs_0_.refs_4_, ...), custom_call_target="tpu_custom_call" | custom-call | flops 1000 | bytes 1000 | tf_op jit(solution)/shard_map/down/pallas_call | solution.py:276
  100.0 3.7 %act.4 = (bf16[224,6144]{1,0:T(8,128)(2,1)}, bf16[224,6144]{1,0:T(8,128)(2,1)}, f32[16,1,384]{2,1,0:T(1,128)S(1)}) custom-call(s32[17]{0:T(128)S(1)} %dynamic-slice_bitcast_fusion.ids_ref, bf16[224,1024]{1,0:T(8,128)(2,1)S(1)} %get-tuple-element.43.refs_0_, ...), custom_call_target="tpu_custom_call", output_to_operand_aliasing={{0}: (10, {}), {1}: (11, {})} | custom-call | flops 1000 | bytes 1000 | tf_op jit(solution)/shard_map/act/pallas_call | solution.py:343
  103.7 1.2 collective-permute-done.15.refs_2_.refs_6_.refs_0_
  104.9 0.9 for_other.6
  105.8 4.1 %collective-permute-start.22 = (bf16[3,224,384]{2,1,0:T(8,128)(2,1)S(1)}, bf16[3,224,384]{2,1,0:T(8,128)(2,1)S(1)}, u32[]{:S(2)}, u32[]{:S(2)}) collective-permute-start(bf16[3,224,384]{2,1,0:T(8,128)(2,1)S(1)} %for_other.6), channel_id=1, source_target_pairs={{0,1},{1,0},{2,3},{3,2},{4,5},{5,4},{6,7},{7,6},{8,9},{9,8},{10,11... | collective-permute-start | bytes 1548296 | tf_op jit(solution)/shard_map/ppermute | solution.py:205
  109.9 1.5 %collective-permute-done.22.refs_8_ = bf16[3,224,384]{2,1,0:T(8,128)(2,1)S(1)} collective-permute-done((bf16[3,224,384]{2,1,0:T(8,128)(2,1)S(1)}, bf16[3,224,384]{2,1,0:T(8,128)(2,1)S(1)}, u32[]{:S(2)}, u32[]{:S(2)}) %collective-permute-start.22) | collective-permute-done | bytes 516128 | tf_op jit(solution)/shard_map/ppermute | solution.py:205
  111.4 0.7 for_other.7
  112.1 0.5 collective-permute-start.23
  112.6 2.2 %down.5 = (bf16[224,1024]{1,0:T(8,128)(2,1)S(1)}, bf16[224,1024]{1,0:T(8,128)(2,1)S(1)}) custom-call(s32[17]{0:T(128)S(1)} %dynamic-slice_bitcast_fusion.ids_ref, bf16[224,7168]{1,0:T(8,128)(2,1)S(1)} %get-tuple-element.71.refs_3_.own_ref, bf16[224,7168]{1,0:T(8,128)(2,1)S(1)} %collective-permute-done.9.give_ref.other_ref, ...), custom_call_target="tpu_custom_call" | custom-call | flops 2000000000 | bytes 1000 | tf_op jit(solution)/shard_map/down/pallas_call | solution.py:276
  114.8 0.0 copy-start.1
  114.8 0.0 copy-start.2
  114.8 3.4 %act.5 = (bf16[224,6144]{1,0:T(8,128)(2,1)}, bf16[224,6144]{1,0:T(8,128)(2,1)}, f32[16,1,384]{2,1,0:T(1,128)S(1)}) custom-call(s32[17]{0:T(128)S(1)} %dynamic-slice_bitcast_fusion.ids_ref, bf16[224,1024]{1,0:T(8,128)(2,1)S(1)} %get-tuple-element.43.refs_0_, ...), custom_call_target="tpu_custom_call", output_to_operand_aliasing={{0}: (11, {}), {1}: (12, {})} | custom-call | flops 1000 | bytes 1000 | tf_op jit(solution)/shard_map/act/pallas_call | solution.py:343
  118.2 0.2 collective-permute-start.24
  118.4 13.1 %all_to_all.17 = f32[16,1,384]{2,1,0:T(1,128)S(1)} all-to-all(f32[16,1,384]{2,1,0:T(1,128)S(1)} %get-tuple-element.74), channel_id=1, replica_groups=mesh['dp'=16,'expert'=8,'tensor'=2] {'dp'}, dimensions={0} | all-to-all | bytes 49152 | tf_op jit(solution)/shard_map/all_to_all | solution.py:486
  131.5 3.3 %all-gather.1 = f32[2,1,384]{2,1,0:T(1,128)S(1)} all-gather(f32[1,1,384]{2,1,0:T(1,128)S(1)} %reshape.21), channel_id=2, replica_groups=mesh['dp'=16,'expert'=8,'tensor'=2] {'tensor'}, dimensions={0}, use_global_device_ids=true | all-gather | bytes 4608 | tf_op jit(solution)/shard_map/all_gather | solution.py:487
  134.8 0.1 all_to_all.12
  134.9 11.0 %all_to_all.18 = f32[8,1,48]{2,1,0:T(1,128)S(1)} all-to-all(f32[8,1,48]{2,1,0:T(1,128)S(1)} %all_to_all.12), channel_id=1, replica_groups=mesh['dp'=16,'expert'=8,'tensor'=2] {'expert'}, dimensions={0} | all-to-all | bytes 3072 | tf_op jit(solution)/shard_map/all_to_all | solution.py:488
  145.9 0.7 unpack.1
  146.6 1.5 %finish.1 = bf16[224,2048]{1,0:T(8,128)(2,1)} custom-call(s32[17]{0:T(128)S(1)} %dynamic-slice_bitcast_fusion.ids_ref, bf16[224,1024]{1,0:T(8,128)(2,1)S(1)} %get-tuple-element.72.mine_ref, bf16[224,1024]{1,0:T(8,128)(2,1)S(1)} %collective-permute-done.24.theirs_ref), custom_call_target="tpu_custom_call" | custom-call | flops 1000 | bytes 1000 | tf_op jit(solution)/shard_map/finish/pallas_call | solution.py:297
  (32 shorter events, 0.1 us)
Async XLA Ops:
  1.3 0.7 copy-start.3
  3.5 0.6 copy-start
  4.2 14.9 %collective-permute-start = (bf16[48,1024]{1,0:T(8,128)(2,1)S(1)}, bf16[48,1024]{1,0:T(8,128)(2,1)S(1)}, u32[]{:S(2)}, u32[]{:S(2)}) collective-permute-start(bf16[48,1024]{1,0:T(8,128)(2,1)S(1)} %get-tuple-element.49), channel_id=1, source_target_pairs={{0,2},{2,4},{4,6},{6,8},{8,10},{10,12},{12,14},{14,0},{1,3},{3,5},... | collective-permute-start | bytes 294920 | tf_op jit(solution)/shard_map/ppermute | solution.py:425
  6.6 12.4 %collective-permute-start.1 = (bf16[48,1024]{1,0:T(8,128)(2,1)S(1)}, bf16[48,1024]{1,0:T(8,128)(2,1)S(1)}, u32[]{:S(2)}, u32[]{:S(2)}) collective-permute-start(bf16[48,1024]{1,0:T(8,128)(2,1)S(1)} %get-tuple-element.51), channel_id=1, source_target_pairs={{0,14},{2,0},{4,2},{6,4},{8,6},{10,8},{12,10},{14,12},{1,15},{3,1}... | collective-permute-start | bytes 294920 | tf_op jit(solution)/shard_map/ppermute | solution.py:425
  10.6 18.0 %collective-permute-start.3 = (bf16[48,1024]{1,0:T(8,128)(2,1)S(1)}, bf16[48,1024]{1,0:T(8,128)(2,1)S(1)}, u32[]{:S(2)}, u32[]{:S(2)}) collective-permute-start(bf16[48,1024]{1,0:T(8,128)(2,1)S(1)} %get-tuple-element.53), channel_id=1, source_target_pairs={{0,6},{2,8},{4,10},{6,12},{8,14},{10,0},{12,2},{14,4},{1,7},{3,9},... | collective-permute-start | bytes 294920 | tf_op jit(solution)/shard_map/ppermute | solution.py:425
  12.2 16.4 %collective-permute-start.4 = (bf16[48,1024]{1,0:T(8,128)(2,1)S(1)}, bf16[48,1024]{1,0:T(8,128)(2,1)S(1)}, u32[]{:S(2)}, u32[]{:S(2)}) collective-permute-start(bf16[48,1024]{1,0:T(8,128)(2,1)S(1)} %get-tuple-element.54), channel_id=1, source_target_pairs={{0,8},{2,10},{4,12},{6,14},{8,0},{10,2},{12,4},{14,6},{1,9},{3,11}... | collective-permute-start | bytes 294920 | tf_op jit(solution)/shard_map/ppermute | solution.py:425
  15.0 13.6 %collective-permute-start.5 = (bf16[48,1024]{1,0:T(8,128)(2,1)S(1)}, bf16[48,1024]{1,0:T(8,128)(2,1)S(1)}, u32[]{:S(2)}, u32[]{:S(2)}) collective-permute-start(bf16[48,1024]{1,0:T(8,128)(2,1)S(1)} %get-tuple-element.55), channel_id=1, source_target_pairs={{0,10},{2,12},{4,14},{6,0},{8,2},{10,4},{12,6},{14,8},{1,11},{3,13... | collective-permute-start | bytes 294920 | tf_op jit(solution)/shard_map/ppermute | solution.py:425
  19.1 9.5 %copy-start.4 = (bf16[48,1024]{1,0:T(8,128)(2,1)}, bf16[48,1024]{1,0:T(8,128)(2,1)S(1)}, u32[]{:S(2)}) copy-start(bf16[48,1024]{1,0:T(8,128)(2,1)S(1)} %collective-permute-done.refs_1_) | copy-start | bytes 294916
  19.1 11.8 %collective-permute-start.6 = (bf16[48,1024]{1,0:T(8,128)(2,1)S(1)}, bf16[48,1024]{1,0:T(8,128)(2,1)S(1)}, u32[]{:S(2)}, u32[]{:S(2)}) collective-permute-start(bf16[48,1024]{1,0:T(8,128)(2,1)S(1)} %get-tuple-element.57), channel_id=1, source_target_pairs={{0,12},{2,14},{4,0},{6,2},{8,4},{10,6},{12,8},{14,10},{1,13},{3,15... | collective-permute-start | bytes 294920 | tf_op jit(solution)/shard_map/ppermute | solution.py:425
  19.1 9.5 %copy-start.5 = (bf16[48,1024]{1,0:T(8,128)(2,1)}, bf16[48,1024]{1,0:T(8,128)(2,1)S(1)}, u32[]{:S(2)}) copy-start(bf16[48,1024]{1,0:T(8,128)(2,1)S(1)} %collective-permute-done.1.refs_7_) | copy-start | bytes 294916
  19.1 11.8 %collective-permute-start.2 = (bf16[48,1024]{1,0:T(8,128)(2,1)S(1)}, bf16[48,1024]{1,0:T(8,128)(2,1)S(1)}, u32[]{:S(2)}, u32[]{:S(2)}) collective-permute-start(bf16[48,1024]{1,0:T(8,128)(2,1)S(1)} %get-tuple-element.52), channel_id=1, source_target_pairs={{0,4},{2,6},{4,8},{6,10},{8,12},{10,14},{12,0},{14,2},{1,5},{3,7},... | collective-permute-start | bytes 294920 | tf_op jit(solution)/shard_map/ppermute | solution.py:425
  28.6 2.3 %copy-start.6 = (bf16[48,1024]{1,0:T(8,128)(2,1)}, bf16[48,1024]{1,0:T(8,128)(2,1)S(1)}, u32[]{:S(2)}) copy-start(bf16[48,1024]{1,0:T(8,128)(2,1)S(1)} %collective-permute-done.3.refs_3_) | copy-start | bytes 294916
  28.6 2.3 %copy-start.7 = (bf16[48,1024]{1,0:T(8,128)(2,1)}, bf16[48,1024]{1,0:T(8,128)(2,1)S(1)}, u32[]{:S(2)}) copy-start(bf16[48,1024]{1,0:T(8,128)(2,1)S(1)} %collective-permute-done.4.refs_4_) | copy-start | bytes 294916
  28.6 2.3 %copy-start.8 = (bf16[48,1024]{1,0:T(8,128)(2,1)}, bf16[48,1024]{1,0:T(8,128)(2,1)S(1)}, u32[]{:S(2)}) copy-start(bf16[48,1024]{1,0:T(8,128)(2,1)S(1)} %collective-permute-done.5.refs_5_) | copy-start | bytes 294916
  30.9 0.6 copy-start.9
  30.9 0.7 copy-start.10
  32.8 25.8 %collective-permute-start.9 = (bf16[224,7168]{1,0:T(8,128)(2,1)S(1)}, bf16[224,7168]{1,0:T(8,128)(2,1)S(1)}, u32[]{:S(2)}, u32[]{:S(2)}) collective-permute-start(bf16[224,7168]{1,0:T(8,128)(2,1)S(1)} %get-tuple-element.71.refs_3_.own_ref), channel_id=1, source_target_pairs={{0,1},{1,0},{2,3},{3,2},{4,5},{5,4},{6,7},{7,6},{8,9},{9,8},{10,11... | collective-permute-start | bytes 9633800 | tf_op jit(solution)/shard_map/ppermute | solution.py:205
  34.6 14.0 %collective-permute-start.7 = (bf16[384,1024]{1,0:T(8,128)(2,1)S(1)}, bf16[384,1024]{1,0:T(8,128)(2,1)S(1)}, u32[]{:S(2)}, u32[]{:S(2)}) collective-permute-start(bf16[384,1024]{1,0:T(8,128)(2,1)S(1)} %in_order.1.refs_0_.refs_4_), channel_id=1, source_target_pairs={{0,16},{1,65},{16,32},{17,81},{32,48},{33,97},{48,0},{49,113},{64,... | collective-permute-start | bytes 2359304 | tf_op jit(solution)/shard_map/ppermute | solution.py:201
  35.9 17.0 %collective-permute-start.10 = (bf16[384,1024]{1,0:T(8,128)(2,1)S(1)}, bf16[384,1024]{1,0:T(8,128)(2,1)S(1)}, u32[]{:S(2)}, u32[]{:S(2)}) collective-permute-start(bf16[384,1024]{1,0:T(8,128)(2,1)S(1)} %in_order.1.refs_0_.refs_4_), channel_id=1, source_target_pairs={{0,48},{1,193},{16,0},{17,209},{32,16},{33,225},{48,32},{49,241},{... | collective-permute-start | bytes 2359304 | tf_op jit(solution)/shard_map/ppermute | solution.py:201
  37.3 18.9 %collective-permute-start.12 = (bf16[384,1024]{1,0:T(8,128)(2,1)S(1)}, bf16[384,1024]{1,0:T(8,128)(2,1)S(1)}, u32[]{:S(2)}, u32[]{:S(2)}) collective-permute-start(bf16[384,1024]{1,0:T(8,128)(2,1)S(1)} %in_order.1.refs_0_.refs_4_), channel_id=1, source_target_pairs={{0,192},{1,49},{16,208},{17,1},{32,224},{33,17},{48,240},{49,33},{... | collective-permute-start | bytes 2359304 | tf_op jit(solution)/shard_map/ppermute | solution.py:201
  39.8 18.8 %collective-permute-start.11 = (bf16[384,1024]{1,0:T(8,128)(2,1)S(1)}, bf16[384,1024]{1,0:T(8,128)(2,1)S(1)}, u32[]{:S(2)}, u32[]{:S(2)}) collective-permute-start(bf16[384,1024]{1,0:T(8,128)(2,1)S(1)} %in_order.1.refs_0_.refs_4_), channel_id=1, source_target_pairs={{0,64},{1,17},{16,80},{17,33},{32,96},{33,49},{48,112},{49,1},{64,... | collective-permute-start | bytes 2359304 | tf_op jit(solution)/shard_map/ppermute | solution.py:201
  48.6 18.5 %collective-permute-start.8 = (bf16[384,1024]{1,0:T(8,128)(2,1)S(1)}, bf16[384,1024]{1,0:T(8,128)(2,1)S(1)}, u32[]{:S(2)}, u32[]{:S(2)}) collective-permute-start(bf16[384,1024]{1,0:T(8,128)(2,1)S(1)} %collective-permute-done.7.refs_1_.a_ref.refs_5_), channel_id=1, source_target_pairs={{0,16},{1,65},{16,32},{17,81},{32,48},{33,97},{48,0},{49,113},{64,... | collective-permute-start | bytes 2359304 | tf_op jit(solution)/shard_map/ppermute | solution.py:201
  53.0 28.5 %collective-permute-start.16 = (bf16[768,1024]{1,0:T(8,128)(2,1)S(1)}, bf16[768,1024]{1,0:T(8,128)(2,1)S(1)}, u32[]{:S(2)}, u32[]{:S(2)}) collective-permute-start(bf16[768,1024]{1,0:T(8,128)(2,1)S(1)} %join.1), channel_id=1, source_target_pairs={{0,64},{1,17},{16,80},{17,33},{32,96},{33,49},{48,112},{49,1},{64,... | collective-permute-start | bytes 4718600 | tf_op jit(solution)/shard_map/ppermute | solution.py:201
  56.2 33.5 %collective-permute-start.20 = (bf16[768,1024]{1,0:T(8,128)(2,1)S(1)}, bf16[768,1024]{1,0:T(8,128)(2,1)S(1)}, u32[]{:S(2)}, u32[]{:S(2)}) collective-permute-start(bf16[768,1024]{1,0:T(8,128)(2,1)S(1)} %join.1), channel_id=1, source_target_pairs={{0,192},{1,49},{16,208},{17,1},{32,224},{33,17},{48,240},{49,33},{... | collective-permute-start | bytes 4718600 | tf_op jit(solution)/shard_map/ppermute | solution.py:201
  60.1 9.8 %collective-permute-start.17 = (bf16[5,224,384]{2,1,0:T(8,128)(2,1)S(1)}, bf16[5,224,384]{2,1,0:T(8,128)(2,1)S(1)}, u32[]{:S(2)}, u32[]{:S(2)}) collective-permute-start(bf16[5,224,384]{2,1,0:T(8,128)(2,1)S(1)} %for_other.4), channel_id=1, source_target_pairs={{0,1},{1,0},{2,3},{3,2},{4,5},{5,4},{6,7},{7,6},{8,9},{9,8},{10,11... | collective-permute-start | bytes 2580488 | tf_op jit(solution)/shard_map/ppermute | solution.py:205
  67.1 22.5 %collective-permute-start.13 = (bf16[384,1024]{1,0:T(8,128)(2,1)S(1)}, bf16[384,1024]{1,0:T(8,128)(2,1)S(1)}, u32[]{:S(2)}, u32[]{:S(2)}) collective-permute-start(bf16[384,1024]{1,0:T(8,128)(2,1)S(1)} %collective-permute-done.8.refs_0_.refs_4_), channel_id=1, source_target_pairs={{0,64},{1,17},{16,80},{17,33},{32,96},{33,49},{48,112},{49,1},{64,... | collective-permute-start | bytes 2359304 | tf_op jit(solution)/shard_map/ppermute | solution.py:201
  68.4 21.3 %collective-permute-start.19 = (bf16[384,1024]{1,0:T(8,128)(2,1)S(1)}, bf16[384,1024]{1,0:T(8,128)(2,1)S(1)}, u32[]{:S(2)}, u32[]{:S(2)}) collective-permute-start(bf16[384,1024]{1,0:T(8,128)(2,1)S(1)} %collective-permute-done.12.refs_4_.refs_8_), channel_id=1, source_target_pairs={{0,192},{1,49},{16,208},{17,1},{32,224},{33,17},{48,240},{49,33},{... | collective-permute-start | bytes 2359304 | tf_op jit(solution)/shard_map/ppermute | solution.py:201
  69.8 23.0 %collective-permute-start.14 = (bf16[384,1024]{1,0:T(8,128)(2,1)S(1)}, bf16[384,1024]{1,0:T(8,128)(2,1)S(1)}, u32[]{:S(2)}, u32[]{:S(2)}) collective-permute-start(bf16[384,1024]{1,0:T(8,128)(2,1)S(1)} %collective-permute-done.8.refs_0_.refs_4_), channel_id=1, source_target_pairs={{0,192},{1,49},{16,208},{17,1},{32,224},{33,17},{48,240},{49,33},{... | collective-permute-start | bytes 2359304 | tf_op jit(solution)/shard_map/ppermute | solution.py:201
  89.6 21.8 %collective-permute-start.18 = (bf16[768,1024]{1,0:T(8,128)(2,1)S(1)}, bf16[768,1024]{1,0:T(8,128)(2,1)S(1)}, u32[]{:S(2)}, u32[]{:S(2)}) collective-permute-start(bf16[768,1024]{1,0:T(8,128)(2,1)S(1)} %collective-permute-done.16.refs_2_.refs_6_), channel_id=1, source_target_pairs={{0,64},{1,17},{16,80},{17,33},{32,96},{33,49},{48,112},{49,1},{64,... | collective-permute-start | bytes 4718600 | tf_op jit(solution)/shard_map/ppermute | solution.py:201
  91.4 8.5 %collective-permute-start.21 = (bf16[6,224,384]{2,1,0:T(8,128)(2,1)S(1)}, bf16[6,224,384]{2,1,0:T(8,128)(2,1)S(1)}, u32[]{:S(2)}, u32[]{:S(2)}) collective-permute-start(bf16[6,224,384]{2,1,0:T(8,128)(2,1)S(1)} %for_other.5), channel_id=1, source_target_pairs={{0,1},{1,0},{2,3},{3,2},{4,5},{5,4},{6,7},{7,6},{8,9},{9,8},{10,11... | collective-permute-start | bytes 3096584 | tf_op jit(solution)/shard_map/ppermute | solution.py:205
  92.8 12.1 %collective-permute-start.15 = (bf16[384,1024]{1,0:T(8,128)(2,1)S(1)}, bf16[384,1024]{1,0:T(8,128)(2,1)S(1)}, u32[]{:S(2)}, u32[]{:S(2)}) collective-permute-start(bf16[384,1024]{1,0:T(8,128)(2,1)S(1)} %collective-permute-done.14.refs_5_.refs_1_), channel_id=1, source_target_pairs={{0,192},{1,49},{16,208},{17,1},{32,224},{33,17},{48,240},{49,33},{... | collective-permute-start | bytes 2359304 | tf_op jit(solution)/shard_map/ppermute | solution.py:201
  105.8 5.6 %collective-permute-start.22 = (bf16[3,224,384]{2,1,0:T(8,128)(2,1)S(1)}, bf16[3,224,384]{2,1,0:T(8,128)(2,1)S(1)}, u32[]{:S(2)}, u32[]{:S(2)}) collective-permute-start(bf16[3,224,384]{2,1,0:T(8,128)(2,1)S(1)} %for_other.6), channel_id=1, source_target_pairs={{0,1},{1,0},{2,3},{3,2},{4,5},{5,4},{6,7},{7,6},{8,9},{9,8},{10,11... | collective-permute-start | bytes 1548296 | tf_op jit(solution)/shard_map/ppermute | solution.py:205
  112.1 2.6 %collective-permute-start.23 = (bf16[2,224,384]{2,1,0:T(8,128)(2,1)S(1)}, bf16[2,224,384]{2,1,0:T(8,128)(2,1)S(1)}, u32[]{:S(2)}, u32[]{:S(2)}) collective-permute-start(bf16[2,224,384]{2,1,0:T(8,128)(2,1)S(1)} %for_other.7), channel_id=1, source_target_pairs={{0,1},{1,0},{2,3},{3,2},{4,5},{5,4},{6,7},{7,6},{8,9},{9,8},{10,11... | collective-permute-start | bytes 1032200 | tf_op jit(solution)/shard_map/ppermute | solution.py:205
  114.8 31.2 %copy-start.1 = (s32[128,2]{0,1:T(2,128)S(1)}, s32[128,2]{0,1:T(2,128)}, u32[]{:S(2)}) copy-start(s32[128,2]{0,1:T(2,128)} %param.12) | copy-start | bytes 3076
  114.8 31.1 %copy-start.2 = (bf16[128,2]{0,1:T(2,128)(2,1)S(1)}, bf16[128,2]{0,1:T(2,128)(2,1)}, u32[]{:S(2)}) copy-start(bf16[128,2]{0,1:T(2,128)(2,1)} %param.13) | copy-start | bytes 1540
  118.2 28.5 %collective-permute-start.24 = (bf16[224,1024]{1,0:T(8,128)(2,1)S(1)}, bf16[224,1024]{1,0:T(8,128)(2,1)S(1)}, u32[]{:S(2)}, u32[]{:S(2)}) collective-permute-start(bf16[224,1024]{1,0:T(8,128)(2,1)S(1)} %get-tuple-element.75), channel_id=1, source_target_pairs={{0,1},{1,0},{2,3},{3,2},{4,5},{5,4},{6,7},{7,6},{8,9},{9,8},{10,11... | collective-permute-start | bytes 1376264 | tf_op jit(solution)/shard_map/ppermute | solution.py:205
